TPU v7x, 512 devices: a whole 4x8x8 slice. The times are simulated.
512 devices in a mesh: boxes: 64 (over y, z), grp: 8 (over x, core).
Axes of the slice: x: 4, y: 8, z: 8, core: 2. Of those that a mesh axis runs over, the one named last changes fastest.
Arguments:
- densities: bfloat16 [1024, 256, 512], P(('boxes', 'grp')), may hold values from -6 to 6
- basis_source: bfloat16 [1024, 64, 256], P(('boxes', 'grp')), may hold values from -0.375 to 0.375
- basis_target: bfloat16 [1024, 64, 256], P(('boxes', 'grp')), may hold values from -0.75 to 0.75
- near_blocks: bfloat16 [1024, 256, 2048], P(('boxes', 'grp')), may hold values from -0.125 to 0.125
- near_leaves: int32 [1024, 8], P(('boxes', 'grp')), may hold values from 0 to 1023, as said below
- near_count: int32 [1024], P(('boxes', 'grp')), may hold values from 1 to 8
- far_coupling: bfloat16 [1024, 64, 2560], P(('boxes', 'grp')), may hold values from -0.125 to 0.125
- far_leaves: int32 [1024, 40], P(('boxes', 'grp')), may hold values from 0 to 1023, as said below
- far_count: int32 [1024], P(('boxes', 'grp')), may hold values from 1 to 40
- leaf_transfer: bfloat16 [1024, 64, 64], P(('boxes', 'grp')), may hold values from -0.375 to 0.375
- box_transfer: bfloat16 [64, 64, 64], replicated, may hold values from -0.375 to 0.375
- box_coupling: bfloat16 [64, 64, 1024], P('boxes'), may hold values from -0.1875 to 0.1875
- box_partners: int32 [64, 16], P('boxes'), may hold values from 0 to 63
- top_coupling: bfloat16 [8, 64, 256], replicated, may hold values from -0.375 to 0.375
- top_partners: int32 [8, 4], replicated, may hold values from 0 to 7
Outputs:
- potential: bfloat16 [1024, 256, 512], P(('boxes', 'grp'))
Inputs may be any that keep to these rules, and one draw needn't show every extreme that they name: `near_leaves`: entry 0 of row t is t itself; every entry s of row t satisfies |s // 2 - t // 2| <= 1, and that distance is reached. `far_leaves`: every entry s of row t satisfies |s // 16 - t // 16| <= 1, and that distance is reached.
All inputs are finite; a program needn't handle non-finite values.
Results may differ from a plain program's by a relative error of at most 0.012.
Values may be sent and summed in bfloat16 or wider, within the bound.
No kernel may reach another device: no remote copies, remote signals or barrier semaphores. Data moves between devices by JAX's collectives and lax.ppermute only.
A program may use at most 64 MiB of HBM per device.

v0:
```python
import jax
import jax.numpy as jnp
from jax import lax
from jax.sharding import PartitionSpec as P

RANK = 64
NEAR_REACH = 1
FAR_REACH = 1
CHILDREN = 8


def from_behind(block, axis, distance):
    devices = range(lax.axis_size(axis))
    route = [(i - distance, i) for i in devices if i - distance in devices]
    return lax.ppermute(block, axis, route)


def masked_rows(source_table, chosen, used_count):
    selected = jnp.take(source_table, chosen, axis=0)
    slot_ids = jnp.arange(chosen.shape[-1], dtype=jnp.int32)
    in_use = slot_ids[None, :] < used_count[:, None]
    selected = jnp.where(in_use[:, :, None, None], selected, jnp.zeros((), selected.dtype))
    return selected.reshape(
        selected.shape[0], selected.shape[1] * selected.shape[2], selected.shape[3]
    )


def shards(
    densities,
    basis_source,
    basis_target,
    near_blocks,
    near_leaves,
    near_count,
    far_coupling,
    far_leaves,
    far_count,
    leaf_transfer,
    box_transfer,
    box_coupling,
    box_partners,
    top_coupling,
    top_partners,
):
    leaf_dev = densities.shape[0]
    groups = lax.axis_size("grp")
    group_leaves = leaf_dev * groups
    box_index = lax.axis_index("boxes")
    device = box_index * groups + lax.axis_index("grp")
    skeleton = jnp.einsum(
        "lkp,lpv->lkv", basis_source, densities, preferred_element_type=jnp.float32
    ).astype(jnp.bfloat16)
    pieces = []
    for offset in range(-NEAR_REACH, NEAR_REACH + 1):
        if offset == 0:
            pieces.append(densities)
        else:
            pieces.append(from_behind(densities, ("boxes", "grp"), -offset))
    near_window = jnp.concatenate(pieces, axis=0)
    grouped = lax.all_gather(skeleton, "grp", axis=0, tiled=True)
    parts_list = []
    for offset in range(-FAR_REACH, FAR_REACH + 1):
        if offset == 0:
            parts_list.append(grouped)
        else:
            parts_list.append(from_behind(grouped, "boxes", -offset))
    far_window = jnp.concatenate(parts_list, axis=0)
    upward = jnp.einsum("lij,ljv->iv", leaf_transfer, skeleton, preferred_element_type=jnp.float32)
    summed = lax.psum(upward, "grp")
    box_skeleton = summed.astype(jnp.bfloat16)
    all_boxes = lax.all_gather(box_skeleton[None], "boxes", axis=0, tiled=True)
    share_cols = all_boxes.shape[-1]
    far_local = far_leaves - (box_index - FAR_REACH) * group_leaves
    far_stack = masked_rows(far_window, far_local, far_count)
    far_field = jnp.einsum(
        "lkq,lqv->lkv", far_coupling, far_stack, preferred_element_type=jnp.float32
    )
    near_local = near_leaves - (device - NEAR_REACH) * leaf_dev
    near_stack = masked_rows(near_window, near_local, near_count)
    near_field = jnp.einsum(
        "lpq,lqv->lpv", near_blocks, near_stack, preferred_element_type=jnp.float32
    )
    children = jnp.einsum(
        "bij,bjv->biv", box_transfer, all_boxes, preferred_element_type=jnp.float32
    )
    top_skeleton = (
        children.reshape(children.shape[0] // CHILDREN, CHILDREN, RANK, share_cols)
        .sum(axis=1)
        .astype(jnp.bfloat16)
    )
    parent = box_index // CHILDREN
    top_row = lax.dynamic_index_in_dim(top_coupling, parent, 0, keepdims=False)
    top_pick = lax.dynamic_index_in_dim(top_partners, parent, 0, keepdims=False)
    top_stack = jnp.take(top_skeleton, top_pick, axis=0).reshape(-1, share_cols)
    top_local = jnp.dot(top_row, top_stack, preferred_element_type=jnp.float32).astype(jnp.bfloat16)
    own_transfer = lax.dynamic_index_in_dim(box_transfer, box_index, 0, keepdims=False)
    box_stack = jnp.take(all_boxes, box_partners[0], axis=0).reshape(-1, share_cols)
    box_value = jnp.dot(box_coupling[0], box_stack, preferred_element_type=jnp.float32)
    box_value = box_value + jnp.einsum(
        "ji,jv->iv", own_transfer, top_local, preferred_element_type=jnp.float32
    )
    box_local = box_value.astype(jnp.bfloat16)
    leaf_value = far_field + jnp.einsum(
        "lji,jv->liv", leaf_transfer, box_local, preferred_element_type=jnp.float32
    )
    leaf_local = leaf_value.astype(jnp.bfloat16)
    potential = (
        jnp.einsum("lkp,lkv->lpv", basis_target, leaf_local, preferred_element_type=jnp.float32)
        + near_field
    )
    return potential.astype(jnp.bfloat16)


def solution(mesh):
    placed = (
        P(("boxes", "grp"), None, None),
        P(("boxes", "grp"), None, None),
        P(("boxes", "grp"), None, None),
        P(("boxes", "grp"), None, None),
        P(("boxes", "grp"), None),
        P(("boxes", "grp")),
        P(("boxes", "grp"), None, None),
        P(("boxes", "grp"), None),
        P(("boxes", "grp")),
        P(("boxes", "grp"), None, None),
        P(),
        P("boxes", None, None),
        P("boxes", None),
        P(),
        P(),
    )
    return jax.shard_map(
        shards,
        mesh=mesh,
        in_specs=placed,
        out_specs=P(("boxes", "grp"), None, None),
        check_vma=False,
    )
```

profile of v0, /device:TPU:2, one launch (start us, length us, event | category | flops | bytes accessed | tf_op | source)
XLA Modules:
  0.0 168.1 jit_solution(18033318773360105706)
XLA Ops:
  6.5 2.1 %convolution_convert_fusion = bf16[2,64,512]{2,1,0:T(8,128)(2,1)} fusion(bf16[2,64,256]{2,1,0:T(8,128)(2,1)} %param.16, bf16[2,256,512]{2,1,0:T(8,128)(2,1)} %param.15), kind=kOutput, calls=%fused_computation.24 | convolution fusion | flops 33619968 | bytes 720896 | tf_op jit(solution)/shard_map/lkp,lpv->lkv/dot_general | solution.py:50
  8.7 1.1 convolution_bitcast_fusion.3
  9.8 27.8 %all-reduce.1 = bf16[64,512]{1,0:T(8,128)(2,1)} all-reduce(f32[64,512]{1,0:T(8,128)S(1)} %convolution_bitcast_fusion.3), channel_id=1, replica_groups=mesh['boxes'=64,'grp'=8] {'grp'}, use_global_device_ids=true, to_apply=%region_0.0 | all-reduce | flops 32768 | bytes 196608 | tf_op jit(solution)/shard_map/psum | solution.py:69
  37.6 1.9 %collective-permute-start.2 = (bf16[2,256,512]{2,1,0:T(8,128)(2,1)}, bf16[2,256,512]{2,1,0:T(8,128)(2,1)S(1)}, u32[]{:S(2)}, u32[]{:S(2)}) collective-permute-start(bf16[2,256,512]{2,1,0:T(8,128)(2,1)} %param.15), channel_id=1, source_target_pairs={{0,1},{1,2},{2,3},{3,4},{4,5},{5,6},{6,7},{7,8},{8,9},{9,10},{10,1... | collective-permute-start | bytes 1572872 | tf_op jit(solution)/shard_map/ppermute | solution.py:15
  39.6 3.6 %collective-permute-start.3 = (bf16[2,256,512]{2,1,0:T(8,128)(2,1)}, bf16[2,256,512]{2,1,0:T(8,128)(2,1)S(1)}, u32[]{:S(2)}, u32[]{:S(2)}) collective-permute-start(bf16[2,256,512]{2,1,0:T(8,128)(2,1)} %param.15), channel_id=1, source_target_pairs={{1,0},{2,1},{3,2},{4,3},{5,4},{6,5},{7,6},{8,7},{9,8},{10,9},{11,1... | collective-permute-start | bytes 1572872 | tf_op jit(solution)/shard_map/ppermute | solution.py:15
  48.4 2.4 %collective-permute-start = (bf16[16,64,512]{2,1,0:T(8,128)(2,1)}, bf16[16,64,512]{2,1,0:T(8,128)(2,1)}, u32[]{:S(2)}, u32[]{:S(2)}) collective-permute-start(bf16[16,64,512]{2,1,0:T(8,128)(2,1)} %all-gather.4.cloned.1.call-done), channel_id=1, source_target_pairs={{0,8},{8,16},{16,24},{24,32},{32,40},{40,48},{48,56},{56,64},{64,7... | collective-permute-start | bytes 3145736 | tf_op jit(solution)/shard_map/ppermute | solution.py:15
  50.7 1.3 collective-permute-start.1
  52.7 2.4 %pad_maximum_fusion.1 = bf16[6,256,512]{2,1,0:T(8,128)(2,1)} fusion(bf16[2,256,512]{2,1,0:T(8,128)(2,1)S(1)} %collective-permute-done.3, bf16[2,256,512]{2,1,0:T(8,128)(2,1)} %param.15, bf16[2,256,512]{2,1,0:T(8,128)(2,1)S(1)} %collective-permute-done.2), kind=kLoop, calls=%fused_computation.15 | loop fusion | flops 1572864 | bytes 3145728 | tf_op jit(solution)/shard_map/concatenate | solution.py:59
  55.1 4.2 %gather_fusion.3 = bf16[16,256,512]{2,1,0:T(8,128)(2,1)} fusion(bf16[6,256,512]{2,1,0:T(8,128)(2,1)} %pad_maximum_fusion.1, s32[1024]{0:T(1024)S(1)} %pad_clamp_fusion), kind=kCustom, calls=%fused_computation.3 | custom fusion | bytes 8388672 | tf_op jit(solution)/shard_map/jit(_take)/gather | solution.py:19
  59.3 6.4 %copy.18 = bf16[2,2048,512]{1,2,0:T(8,128)(2,1)} copy(bf16[2,2048,512]{2,1,0:T(8,128)(2,1)} %bitcast.75) | data formatting | bytes 8388608 | tf_op jit(solution)/shard_map/jit(_take)/gather | solution.py:19
  65.7 6.7 %collective-permute-done = bf16[16,64,512]{2,1,0:T(8,128)(2,1)} collective-permute-done((bf16[16,64,512]{2,1,0:T(8,128)(2,1)}, bf16[16,64,512]{2,1,0:T(8,128)(2,1)}, u32[]{:S(2)}, u32[]{:S(2)}) %collective-permute-start) | collective-permute-done | bytes 1048608 | tf_op jit(solution)/shard_map/ppermute | solution.py:15
  72.4 5.7 %collective-permute-done.1 = bf16[16,64,512]{2,1,0:T(8,128)(2,1)} collective-permute-done((bf16[16,64,512]{2,1,0:T(8,128)(2,1)}, bf16[16,64,512]{2,1,0:T(8,128)(2,1)}, u32[]{:S(2)}, u32[]{:S(2)}) %collective-permute-start.1) | collective-permute-done | bytes 1048608 | tf_op jit(solution)/shard_map/ppermute | solution.py:15
  78.0 3.1 %pad_maximum_fusion = bf16[48,64,512]{2,1,0:T(8,128)(2,1)} fusion(bf16[16,64,512]{2,1,0:T(8,128)(2,1)} %collective-permute-done.1, bf16[16,64,512]{2,1,0:T(8,128)(2,1)S(1)} %copy-done.2, bf16[16,64,512]{2,1,0:T(8,128)(2,1)} %collective-permute-done), kind=kLoop, calls=%fused_computation.12 | loop fusion | flops 3145728 | bytes 6291456 | tf_op jit(solution)/shard_map/concatenate | solution.py:67
  81.1 7.6 %gather_fusion = bf16[80,64,512]{2,1,0:T(8,128)(2,1)} fusion(bf16[48,64,512]{2,1,0:T(8,128)(2,1)} %pad_maximum_fusion, s32[1024]{0:T(1024)S(1)} %pad_clamp_fusion.3), kind=kCustom, calls=%fused_computation | custom fusion | bytes 10486080 | tf_op jit(solution)/shard_map/jit(_take)/gather | solution.py:19
  88.7 7.3 %fusion = bf16[2,2560,512]{2,1,0:T(8,128)(2,1)} fusion(pred[2,2560]{1,0:T(4,128)(4,1)S(1)} %broadcast_in_dim.97, pred[2,2560]{1,0:T(4,128)(4,1)S(1)} %broadcast_in_dim.94, bf16[2,2560,512]{2,1,0:T(8,128)(2,1)} %bitcast.74), kind=kLoop, calls=%fused_computation.6 | loop fusion | flops 5242880 | bytes 10496000 | tf_op jit(solution)/shard_map/jit(_where)/select_n | solution.py:22
  96.0 42.1 %all-gather.6.cloned.1.call-done = bf16[4096,512]{1,0:T(8,128)(2,1)} async-done(((bf16[64,512]{1,0:T(8,128)(2,1)}), bf16[4096,512]{1,0:T(8,128)(2,1)}) %all-gather.6.cloned.1.call-update) | async-done | bytes 4194320 | tf_op jit(solution)/shard_map/all_gather | solution.py:71
  138.1 4.3 %bitcast_reduce_fusion = bf16[8,64,512]{2,1,0:T(8,128)(2,1)} fusion(bf16[64,64,64]{2,1,0:T(8,128)(2,1)S(1)} %copy-done.1, bf16[64,64,512]{2,1,0:T(8,128)(2,1)} %bitcast.76), kind=kOutput, calls=%fused_computation.4 | convolution fusion | flops 270270464 | bytes 5242880 | tf_op jit(solution)/shard_map/bij,bjv->biv/dot_general | solution.py:83
  142.4 2.8 %gather_fusion.1 = bf16[16,64,512]{2,1,0:T(8,128)(2,1)S(1)} fusion(bf16[64,64,512]{2,1,0:T(8,128)(2,1)} %bitcast.77, s32[1024]{0:T(1024)S(1)} %pad_clamp_fusion.2), kind=kCustom, calls=%fused_computation.1 | custom fusion | bytes 2097216 | tf_op jit(solution)/shard_map/jit(_take)/gather | solution.py:97
  145.2 1.6 gather_fusion.2
  147.8 1.4 convolution_bitcast_fusion.1
  149.2 1.4 fusion.20
  150.8 4.0 %fusion.21 = f32[2,512,256]{2,1,0:T(8,128)S(1)} fusion(bf16[2,64,256]{2,1,0:T(8,128)(2,1)S(1)} %copy-done.4, f32[2,64,512]{2,1,0:T(8,128)S(1)} %convolution_bitcast_fusion, bf16[2,64,2560]{2,1,0:T(8,128)(2,1)} %param.21, bf16[2,2560,512]{2,1,0:T(8,128)(2,1)} %fusion), kind=kOutput, calls=%fused_computation.29 | convolution fusion | flops 369229824 | bytes 7274496 | tf_op jit(solution)/shard_map/lkp,lkv->lpv/dot_general | solution.py:108
  154.9 4.3 %fusion.14 = bf16[2,256,512]{1,2,0:T(8,128)(2,1)} fusion(f32[2,512,256]{2,1,0:T(8,128)S(1)} %fusion.21, bf16[2,256,2048]{2,1,0:T(8,128)(2,1)S(1)} %copy-done, bf16[2,2048,512]{1,2,0:T(8,128)(2,1)} %copy.18, pred[2,2048]{1,0:T(4,128)(4,1)S(1)} %bitcast.80, pred[2,2048]{1,0:T(4,128)(4,1)S(1)} %bitcast.81), kind=kOutput, calls=%fused_computation.18 | convolution fusion | flops 1078460416 | bytes 7872512 | tf_op jit(solution)/shard_map/lpq,lqv->lpv/dot_general | solution.py:80
  159.2 2.0 %copy.19 = bf16[2,256,512]{2,1,0:T(8,128)(2,1)} copy(bf16[2,256,512]{1,2,0:T(8,128)(2,1)} %fusion.14) | data formatting | bytes 1048576 | tf_op jit(solution)/shard_map/convert_element_type | solution.py:111
  (43 shorter events, 7.0 us)
Async XLA Ops:
  6.5 148.4 %copy-start = (bf16[2,256,2048]{2,1,0:T(8,128)(2,1)S(1)}, bf16[2,256,2048]{2,1,0:T(8,128)(2,1)}, u32[]{:S(2)}) copy-start(bf16[2,256,2048]{2,1,0:T(8,128)(2,1)} %param.18) | copy-start | bytes 6291460
  6.5 41.8 %all-gather.4.cloned.1.call-start = ((), (), s32[]{:S(2)}) async-start(), calls=%async_computation | async-start | bytes 1179648 | tf_op jit(solution)/shard_map/all_gather | solution.py:60
  8.6 129.4 %all-gather.6.cloned.1.call-start = ((), (), s32[]{:S(2)}) async-start(), calls=%async_computation.1 | async-start | bytes 4259840 | tf_op jit(solution)/shard_map/all_gather | solution.py:71
  37.6 15.1 %collective-permute-start.2 = (bf16[2,256,512]{2,1,0:T(8,128)(2,1)}, bf16[2,256,512]{2,1,0:T(8,128)(2,1)S(1)}, u32[]{:S(2)}, u32[]{:S(2)}) collective-permute-start(bf16[2,256,512]{2,1,0:T(8,128)(2,1)} %param.15), channel_id=1, source_target_pairs={{0,1},{1,2},{2,3},{3,4},{4,5},{5,6},{6,7},{7,8},{8,9},{9,10},{10,1... | collective-permute-start | bytes 1572872 | tf_op jit(solution)/shard_map/ppermute | solution.py:15
  39.6 13.2 %collective-permute-start.3 = (bf16[2,256,512]{2,1,0:T(8,128)(2,1)}, bf16[2,256,512]{2,1,0:T(8,128)(2,1)S(1)}, u32[]{:S(2)}, u32[]{:S(2)}) collective-permute-start(bf16[2,256,512]{2,1,0:T(8,128)(2,1)} %param.15), channel_id=1, source_target_pairs={{1,0},{2,1},{3,2},{4,3},{5,4},{6,5},{7,6},{8,7},{9,8},{10,9},{11,1... | collective-permute-start | bytes 1572872 | tf_op jit(solution)/shard_map/ppermute | solution.py:15
  48.4 24.0 %collective-permute-start = (bf16[16,64,512]{2,1,0:T(8,128)(2,1)}, bf16[16,64,512]{2,1,0:T(8,128)(2,1)}, u32[]{:S(2)}, u32[]{:S(2)}) collective-permute-start(bf16[16,64,512]{2,1,0:T(8,128)(2,1)} %all-gather.4.cloned.1.call-done), channel_id=1, source_target_pairs={{0,8},{8,16},{16,24},{24,32},{32,40},{40,48},{48,56},{56,64},{64,7... | collective-permute-start | bytes 3145736 | tf_op jit(solution)/shard_map/ppermute | solution.py:15
  50.7 27.3 %collective-permute-start.1 = (bf16[16,64,512]{2,1,0:T(8,128)(2,1)}, bf16[16,64,512]{2,1,0:T(8,128)(2,1)}, u32[]{:S(2)}, u32[]{:S(2)}) collective-permute-start(bf16[16,64,512]{2,1,0:T(8,128)(2,1)} %all-gather.4.cloned.1.call-done), channel_id=1, source_target_pairs={{8,0},{16,8},{24,16},{32,24},{40,32},{48,40},{56,48},{64,56},{72,6... | collective-permute-start | bytes 3145736 | tf_op jit(solution)/shard_map/ppermute | solution.py:15
  59.3 18.7 %copy-start.2 = (bf16[16,64,512]{2,1,0:T(8,128)(2,1)S(1)}, bf16[16,64,512]{2,1,0:T(8,128)(2,1)}, u32[]{:S(2)}) copy-start(bf16[16,64,512]{2,1,0:T(8,128)(2,1)} %all-gather.4.cloned.1.call-done) | copy-start | bytes 3145732
  88.7 49.4 %copy-start.1 = (bf16[64,64,64]{2,1,0:T(8,128)(2,1)S(1)}, bf16[64,64,64]{2,1,0:T(8,128)(2,1)}, u32[]{:S(2)}) copy-start(bf16[64,64,64]{2,1,0:T(8,128)(2,1)} %param.25) | copy-start | bytes 1572868
  142.4 8.2 %copy-start.3 = (bf16[2,64,64]{2,1,0:T(8,128)(2,1)S(1)}, bf16[2,64,64]{2,1,0:T(8,128)(2,1)}, u32[]{:S(2)}) copy-start(bf16[2,64,64]{2,1,0:T(8,128)(2,1)} %param.24) | copy-start | bytes 49156
  142.4 8.5 %copy-start.4 = (bf16[2,64,256]{2,1,0:T(8,128)(2,1)S(1)}, bf16[2,64,256]{2,1,0:T(8,128)(2,1)}, u32[]{:S(2)}) copy-start(bf16[2,64,256]{2,1,0:T(8,128)(2,1)} %param.17) | copy-start | bytes 196612
Sparse Core Ops, SparseCore 0:
  9.5 32.0 all-gather.3
  44.7 93.3 all-gather.5
where the time goes:
time: 169 us; the launch traced here: 168 us
  waiting for transfers between devices  54.5 us (32%)
  blocking collectives  27.8 us (16%)
  local copies, waits for them, and re-layouts  26.2 us (16%)
  matrix products  18.9 us (11%)
  other arithmetic  17.9 us (11%)
  between operations  13.6 us (8%)
  starting transfers between devices  9.26 us (5%)
    all_gather x1, waiting for transfers between devices, shards(): all_boxes = lax.all_gather(box_skeleton[None], 'boxes', axis=0, tiled=True)  42.1 us
    psum x1, blocking collectives, shards(): summed = lax.psum(upward, 'grp')  27.8 us
    gather x3, local copies, waits for them, and re-layouts, masked_rows(): selected = jnp.take(source_table, chosen, axis=0)  18.1 us
    ppermute x4, waiting for transfers between devices, from_behind(): return lax.ppermute(block, axis, route)  12.4 us
    ppermute x4, starting transfers between devices, from_behind(): return lax.ppermute(block, axis, route)  9.21 us
    select_n x1, other arithmetic, masked_rows(): jnp.where(in_use[:, :, None, None], selected, jnp.zeros((), selected.dtype))  7.3 us
    dot_general x1, matrix products, shards(): jnp.einsum('bij,bjv->biv', box_transfer, all_boxes, preferred_element_typ...  4.32 us
    dot_general x1, matrix products, shards(): jnp.einsum('lpq,lqv->lpv', near_blocks, near_stack, preferred_element_typ...  4.28 us
  transfers between devices with their start and end apart: 6, of which 3 were waited for; matrix products, arithmetic and copies ran while one was open for 22% of the time, Pallas kernels for 0%

commit v1 on v0

v1 whole, which is shorter than its diff:
```python
import functools

import jax
import jax.numpy as jnp
from jax import lax
from jax.experimental import pallas as pl
from jax.experimental.pallas import tpu as pltpu
from jax.sharding import Mesh, PartitionSpec as P

RANK = 64
CHILDREN = 8
F32 = jnp.float32
BF16 = jnp.bfloat16
VMEM = pltpu.VMEM
SMEM = pltpu.SMEM


def dot(a, b):
    return jnp.dot(a, b, preferred_element_type=F32)


def dot_t(a, b):
    return lax.dot_general(a, b, (((0,), (0,)), ((), ())), preferred_element_type=F32)


def call(body, out_shape, spaces, flops, moved, scratch=(), limit=32 << 20):
    outs = jax.tree.map(lambda _: pl.BlockSpec(memory_space=VMEM), out_shape)
    return pl.pallas_call(
        body,
        out_shape=out_shape,
        in_specs=[pl.BlockSpec(memory_space=s) for s in spaces],
        out_specs=outs,
        scratch_shapes=list(scratch),
        compiler_params=pltpu.CompilerParams(vmem_limit_bytes=limit),
        cost_estimate=pl.CostEstimate(flops=flops, bytes_accessed=moved, transcendentals=0),
    )


def upward_body(groups, basis, densities, transfer, skeleton, pieces):
    total = None
    for leaf in range(densities.shape[0]):
        value = dot(basis[leaf], densities[leaf]).astype(BF16)
        skeleton[leaf] = value
        term = dot(transfer[leaf], value)
        total = term if total is None else total + term
    total = total.astype(BF16)
    rows, cols = pieces.shape[1:]
    for piece in range(groups):
        top, left = (piece % 2) * rows, (piece // 2) * cols
        pieces[piece] = total[top : top + rows, left : left + cols]


def spread_body(arrived, copies):
    total = arrived[0].astype(F32)
    for piece in range(1, arrived.shape[0]):
        total = total + arrived[piece].astype(F32)
    total = total.astype(BF16)
    for target in range(copies.shape[0]):
        copies[target] = total


def weight_body(coupling, transfer, top_coupling, top_partners, weights):
    box = lax.axis_index("boxes")
    half = lax.axis_index("core")
    parent = box // CHILDREN
    own = transfer[box]
    lefts = dot_t(own, top_coupling[parent])
    near = coupling.shape[-1]

    def keep(value):
        lane = lax.broadcasted_iota(jnp.int32, value.shape, 1)
        return jnp.where((lane // (RANK // 2)) % 2 == half, value, 0.0).astype(BF16)

    weights[:, :near] = keep(coupling[0].astype(F32))
    span = CHILDREN * RANK
    for slot in range(top_partners.shape[1]):
        top = top_partners[parent, slot]
        left = lefts[:, slot * RANK : (slot + 1) * RANK].astype(BF16)
        wide = jnp.concatenate([dot(left, transfer[top * CHILDREN + k]) for k in range(CHILDREN)], axis=1)
        weights[:, near + slot * span : near + (slot + 1) * span] = keep(wide)


def box_body(weights, boxes, box_partners, top_partners, copies):
    parent = lax.axis_index("boxes") // CHILDREN
    sources = [box_partners[0, j] for j in range(box_partners.shape[1])]
    for slot in range(top_partners.shape[1]):
        first = top_partners[parent, slot] * CHILDREN
        sources += [first + k for k in range(CHILDREN)]
    total = None
    step = 4
    for at in range(0, len(sources), step):
        rows = []
        for source in sources[at : at + step]:
            value = boxes[source]
            rows += [value, value]
        term = dot(weights[:, at * RANK : (at + step) * RANK], jnp.concatenate(rows, axis=0))
        total = term if total is None else total + term
    total = total.astype(BF16)
    for target in range(copies.shape[0]):
        copies[target] = total


def trio_body(behind, own, ahead, copies):
    for target in range(copies.shape[0]):
        copies[target, 0] = behind[...]
        copies[target, 1] = own[...]
        copies[target, 2] = ahead[...]


def near_body(device_of, blocks, behind, own, ahead, leaves, count, out, window, sems):
    loads = [
        pltpu.make_async_copy(part, window.at[pl.ds(2 * i, 2)], sems.at[i])
        for i, part in enumerate((behind, own, ahead))
    ]
    for load in loads:
        load.start()
    for load in loads:
        load.wait()
    base = (device_of() - 1) * own.shape[0]
    points = own.shape[1]
    for leaf in range(own.shape[0]):
        total = None
        for j in range(leaves.shape[1]):
            value = window[leaves[leaf, j] - base]
            value = jnp.where(j < count[leaf], value, jnp.zeros_like(value))
            term = dot(blocks[leaf, :, j * points : (j + 1) * points], value)
            total = term if total is None else total + term
        out[leaf] = total


def leaf_body(
    group_leaves, far_coupling, mine, other, far_leaves, far_count, local, transfer, target, near, out, window, sems
):
    half = lax.axis_index("core")
    loads = [
        pltpu.make_async_copy(mine, window.at[half], sems.at[0]),
        pltpu.make_async_copy(other, window.at[1 - half], sems.at[1]),
    ]
    for load in loads:
        load.start()
    parts = []
    for piece in range(0, local.shape[0], 2):
        parts.append(local[piece].astype(F32) + local[piece + 1].astype(F32))
    box_local = jnp.concatenate(parts, axis=1).astype(BF16)
    base = (lax.axis_index("boxes") - 1) * group_leaves
    for load in loads:
        load.wait()
    step = 4
    leaf_dev = transfer.shape[0]
    for leaf in range(leaf_dev):
        total = dot_t(transfer[leaf], box_local)
        for at in range(0, far_leaves.shape[1], step):
            rows = []
            for j in range(at, at + step):
                source = far_leaves[leaf, j] - base
                box, within = source // group_leaves, source % group_leaves
                chip, side, which = within // (2 * leaf_dev), (within // leaf_dev) % 2, within % leaf_dev
                value = window[side, chip, box, which]
                rows.append(jnp.where(j < far_count[leaf], value, jnp.zeros_like(value)))
            total = total + dot(
                far_coupling[leaf, :, at * RANK : (at + step) * RANK], jnp.concatenate(rows, axis=0)
            )
        out[leaf] = (dot_t(target[leaf], total.astype(BF16)) + near[leaf]).astype(BF16)


def shift(block, axis, distance):
    devices = range(lax.axis_size(axis))
    route = [(i - distance, i) for i in devices if i - distance in devices]
    return lax.ppermute(block, axis, route)


def shards(
    densities,
    basis_source,
    basis_target,
    near_blocks,
    near_leaves,
    near_count,
    far_coupling,
    far_leaves,
    far_count,
    leaf_transfer,
    box_transfer,
    box_coupling,
    box_partners,
    top_coupling,
    top_partners,
):
    chips, cores = lax.axis_size("x"), lax.axis_size("core")
    groups = chips * cores
    boxes = lax.axis_size("boxes")
    leaf_dev, points, vectors = densities.shape
    cols, rows = vectors // chips, RANK // cores
    grp = ("x", "core")
    line = ("boxes", "x", "core")

    skeleton, pieces = call(
        functools.partial(upward_body, groups),
        (
            jax.ShapeDtypeStruct((leaf_dev, RANK, vectors), BF16),
            jax.ShapeDtypeStruct((groups, rows, cols), BF16),
        ),
        [VMEM] * 3,
        2 * leaf_dev * RANK * vectors * (points + RANK),
        densities.size * 2,
    )(basis_source, densities, leaf_transfer)
    arrived = lax.all_to_all(pieces, grp, 0, 0, tiled=True)

    behind_skeleton = shift(skeleton, "boxes", 1)
    ahead_skeleton = shift(skeleton, "boxes", -1)

    spread = call(
        spread_body,
        jax.ShapeDtypeStruct((boxes, rows, cols), BF16),
        [VMEM],
        groups * rows * cols,
        boxes * rows * cols * 2,
    )(arrived)
    all_boxes = lax.all_to_all(spread, "boxes", 0, 0, tiled=True)

    trio = call(
        trio_body,
        jax.ShapeDtypeStruct((chips, 3, leaf_dev, RANK, vectors), BF16),
        [VMEM] * 3,
        0,
        chips * 3 * skeleton.size * 2,
    )(behind_skeleton, skeleton, ahead_skeleton)
    mine = lax.all_to_all(trio, "x", 0, 0, tiled=True)
    other = lax.ppermute(mine, "core", [(0, 1), (1, 0)])

    behind = shift(densities, line, 1)
    ahead = shift(densities, line, -1)

    sources = box_partners.shape[1] + top_partners.shape[1] * CHILDREN
    weights = call(
        weight_body,
        jax.ShapeDtypeStruct((RANK, sources * RANK), BF16),
        [VMEM, VMEM, VMEM, SMEM],
        2 * RANK * RANK * RANK * sources,
        box_transfer.size * 2,
    )(box_coupling, box_transfer, top_coupling, top_partners)
    local = call(
        box_body,
        jax.ShapeDtypeStruct((groups, RANK, cols), BF16),
        [VMEM, VMEM, SMEM, SMEM],
        2 * RANK * RANK * sources * cols,
        all_boxes.size * 2,
    )(weights, all_boxes, box_partners, top_partners)
    local = lax.all_to_all(local, grp, 0, 0, tiled=True)

    def device_of():
        return (lax.axis_index("boxes") * chips + lax.axis_index("x")) * cores + lax.axis_index("core")

    near_field = call(
        functools.partial(near_body, device_of),
        jax.ShapeDtypeStruct((leaf_dev, points, vectors), F32),
        [VMEM, pl.ANY, pl.ANY, pl.ANY, SMEM, SMEM],
        2 * near_blocks.size * vectors,
        near_blocks.size * 2 + 5 * densities.size * 2,
        (VMEM((3 * leaf_dev, points, vectors), BF16), pltpu.SemaphoreType.DMA((3,))),
    )(near_blocks, behind, densities, ahead, near_leaves, near_count)

    return call(
        functools.partial(leaf_body, groups * leaf_dev),
        jax.ShapeDtypeStruct(densities.shape, BF16),
        [VMEM, pl.ANY, pl.ANY, SMEM, SMEM, VMEM, VMEM, VMEM, VMEM],
        2 * far_coupling.size * vectors,
        2 * mine.size * 2 + 3 * densities.size * 2,
        (VMEM((2,) + mine.shape, BF16), pltpu.SemaphoreType.DMA((2,))),
    )(far_coupling, mine, other, far_leaves, far_count, local, leaf_transfer, basis_target, near_field)


def solution(mesh):
    boxes, groups = mesh.devices.shape
    fine = Mesh(mesh.devices.reshape(boxes, groups // 2, 2), ("boxes", "x", "core"))
    line = ("boxes", "x", "core")
    leaf = P(line, None, None)
    placed = (
        leaf,
        leaf,
        leaf,
        leaf,
        P(line, None),
        P(line),
        leaf,
        P(line, None),
        P(line),
        leaf,
        P(),
        P("boxes", None, None),
        P("boxes", None),
        P(),
        P(),
    )
    return jax.shard_map(shards, mesh=fine, in_specs=placed, out_specs=leaf, check_vma=False)
```

time: 169 us -> 105 us (0.62)
  the two profiles are of different devices: /device:TPU:2 before, /device:TPU:1 now
where the time goes in v1:
time: 105 us; the launch traced here: 104 us
  starting transfers between devices  46.9 us (45%)
  blocking collectives  26.8 us (26%)
  Pallas kernels  12.1 us (12%)
  waiting for transfers between devices  11.2 us (11%)
  local copies, waits for them, and re-layouts  6.65 us (6%)
    all_to_all x1, blocking collectives, shards(): mine = lax.all_to_all(trio, 'x', 0, 0, tiled=True)  19.6 us
    all_to_all x1, starting transfers between devices, shards(): all_boxes = lax.all_to_all(spread, 'boxes', 0, 0, tiled=True)  19.5 us
    ppermute x4, starting transfers between devices, shift(): return lax.ppermute(block, axis, route)  11.9 us
    all_to_all x1, waiting for transfers between devices, shards(): all_boxes = lax.all_to_all(spread, 'boxes', 0, 0, tiled=True)  8.67 us
    ppermute x1, starting transfers between devices, shards(): other = lax.ppermute(mine, 'core', [(0, 1), (1, 0)])  8.19 us
    all_to_all x1, starting transfers between devices, shards(): local = lax.all_to_all(local, grp, 0, 0, tiled=True)  7.38 us
    all_to_all x1, blocking collectives, shards(): arrived = lax.all_to_all(pieces, grp, 0, 0, tiled=True)  7.23 us
    unnamed x35, local copies, waits for them, and re-layouts  6.65 us
  transfers between devices with their start and end apart: 7, of which 4 were waited for; matrix products, arithmetic and copies ran while one was open for 0% of the time, Pallas kernels for 6%

profile of v1, /device:TPU:1, one launch (start us, length us, event | category | flops | bytes accessed | tf_op | source)
XLA Modules:
  0.0 103.8 jit_solution(3480171613414688214)
XLA Ops:
  0.0 1.0 %copy-done.1 = bf16[2,256,512]{2,1,0:T(8,128)(2,1)S(1)} copy-done((bf16[2,256,512]{2,1,0:T(8,128)(2,1)S(1)}, bf16[2,256,512]{2,1,0:T(8,128)(2,1)}, u32[]{:S(2)}) %copy-start.1) | copy-done | bytes 524312
  1.0 0.8 copy-done.6
  1.8 0.8 copy-done.10
  3.0 1.3 %collective-permute-start.1 = (bf16[2,64,512]{2,1,0:T(8,128)(2,1)S(1)}, bf16[2,64,512]{2,1,0:T(8,128)(2,1)S(1)}, u32[]{:S(2)}, u32[]{:S(2)}) collective-permute-start(bf16[2,64,512]{2,1,0:T(8,128)(2,1)S(1)} %get-tuple-element.7.own), channel_id=1, source_target_pairs={{8,0},{16,8},{24,16},{32,24},{40,32},{48,40},{56,48},{64,56},{72,6... | collective-permute-start | bytes 393224 | tf_op jit(solution)/shard_map/ppermute | solution.py:169
  4.3 5.5 %collective-permute-start = (bf16[2,64,512]{2,1,0:T(8,128)(2,1)S(1)}, bf16[2,64,512]{2,1,0:T(8,128)(2,1)S(1)}, u32[]{:S(2)}, u32[]{:S(2)}) collective-permute-start(bf16[2,64,512]{2,1,0:T(8,128)(2,1)S(1)} %get-tuple-element.7.own), channel_id=1, source_target_pairs={{0,8},{8,16},{16,24},{24,32},{32,40},{40,48},{48,56},{56,64},{64,7... | collective-permute-start | bytes 393224 | tf_op jit(solution)/shard_map/ppermute | solution.py:169
  9.8 0.4 collective-permute-done.1.ahead
  10.2 1.5 %collective-permute-done.behind = bf16[2,64,512]{2,1,0:T(8,128)(2,1)S(1)} collective-permute-done((bf16[2,64,512]{2,1,0:T(8,128)(2,1)S(1)}, bf16[2,64,512]{2,1,0:T(8,128)(2,1)S(1)}, u32[]{:S(2)}, u32[]{:S(2)}) %collective-permute-start) | collective-permute-done | bytes 131104 | tf_op jit(solution)/shard_map/ppermute | solution.py:169
  11.8 19.6 %all_to_all.20.mine = bf16[4,3,2,64,512]{4,3,2,1,0:T(8,128)(2,1)S(1)} all-to-all(bf16[4,3,2,64,512]{4,3,2,1,0:T(8,128)(2,1)S(1)} %shard_map.146), channel_id=1, replica_groups=mesh['boxes'=64,'x'=4,'core'=2] {'x'}, dimensions={0} | all-to-all | bytes 3145728 | tf_op jit(solution)/shard_map/all_to_all | solution.py:228
  31.4 8.2 %collective-permute-start.2 = (bf16[4,3,2,64,512]{4,3,2,1,0:T(8,128)(2,1)S(1)}, bf16[4,3,2,64,512]{4,3,2,1,0:T(8,128)(2,1)}, u32[]{:S(2)}, u32[]{:S(2)}) collective-permute-start(bf16[4,3,2,64,512]{4,3,2,1,0:T(8,128)(2,1)S(1)} %all_to_all.20.mine), channel_id=1, source_target_pairs={{0,1},{1,0},{2,3},{3,2},{4,5},{5,4},{6,7},{7,6},{8,9},{9,8},{10,11... | collective-permute-start | bytes 4718600 | tf_op jit(solution)/shard_map/ppermute | solution.py:229
  39.6 7.2 %all_to_all.21.arrived = bf16[8,32,128]{2,1,0:T(8,128)(2,1)S(1)} all-to-all(bf16[8,32,128]{2,1,0:T(8,128)(2,1)S(1)} %get-tuple-element.8), channel_id=1, replica_groups=mesh['boxes'=64,'x'=4,'core'=2] {'x','core'}, dimensions={0} | all-to-all | bytes 131072 | tf_op jit(solution)/shard_map/all_to_all | solution.py:207
  46.8 0.8 shard_map.148
  47.6 19.5 %all-to-all-start.2 = ((bf16[64,32,128]{2,1,0:T(8,128)(2,1)}), bf16[64,32,128]{2,1,0:T(8,128)(2,1)S(1)}, u32[]{:S(2)}, u32[]{:S(2)}) async-start(bf16[64,32,128]{2,1,0:T(8,128)(2,1)} %shard_map.148), calls=%async_computation.2 | async-start | bytes 1048576 | tf_op jit(solution)/shard_map/all_to_all | solution.py:219
  67.1 3.1 %collective-permute-start.3 = (bf16[2,256,512]{2,1,0:T(8,128)(2,1)S(1)}, bf16[2,256,512]{2,1,0:T(8,128)(2,1)}, u32[]{:S(2)}, u32[]{:S(2)}) collective-permute-start(bf16[2,256,512]{2,1,0:T(8,128)(2,1)S(1)} %copy-done.2), channel_id=1, source_target_pairs={{0,1},{1,2},{2,3},{3,4},{4,5},{5,6},{6,7},{7,8},{8,9},{9,10},{10,1... | collective-permute-start | bytes 1572872 | tf_op jit(solution)/shard_map/ppermute | solution.py:169
  70.3 2.0 %collective-permute-start.4 = (bf16[2,256,512]{2,1,0:T(8,128)(2,1)S(1)}, bf16[2,256,512]{2,1,0:T(8,128)(2,1)}, u32[]{:S(2)}, u32[]{:S(2)}) collective-permute-start(bf16[2,256,512]{2,1,0:T(8,128)(2,1)S(1)} %copy-done.2), channel_id=1, source_target_pairs={{1,0},{2,1},{3,2},{4,3},{5,4},{6,5},{7,6},{8,7},{9,8},{10,9},{11,1... | collective-permute-start | bytes 1572872 | tf_op jit(solution)/shard_map/ppermute | solution.py:169
  72.4 1.2 %copy-done.3 = bf16[64,64,64]{2,1,0:T(8,128)(2,1)S(1)} copy-done((bf16[64,64,64]{2,1,0:T(8,128)(2,1)S(1)}, bf16[64,64,64]{2,1,0:T(8,128)(2,1)}, u32[]{:S(2)}) %copy-start.3) | copy-done | bytes 524312
  73.6 1.2 %shard_map.147.weights = bf16[64,3072]{1,0:T(8,128)(2,1)S(1)} custom-call(bf16[1,64,1024]{2,1,0:T(8,128)(2,1)S(1)} %copy-done.8, bf16[64,64,64]{2,1,0:T(8,128)(2,1)S(1)} %copy-done.3, bf16[8,64,256]{2,1,0:T(8,128)(2,1)S(1)} %copy-done.5, s32[8,4]{1,0:T(8,128)S(1)} %copy.16.top_partners), custom_call_target="tpu_custom_call" | custom-call | flops 25165824 | bytes 524288 | tf_op jit(solution)/shard_map/pallas_call | solution.py:235
  74.7 8.7 %all-to-all-done.2.boxes = bf16[64,32,128]{2,1,0:T(8,128)(2,1)S(1)} async-done(((bf16[64,32,128]{2,1,0:T(8,128)(2,1)}), bf16[64,32,128]{2,1,0:T(8,128)(2,1)S(1)}, u32[]{:S(2)}, u32[]{:S(2)}) %all-to-all-start.2) | async-done | bytes 524320 | tf_op jit(solution)/shard_map/all_to_all | solution.py:219
  83.4 1.5 %shard_map.149 = bf16[8,64,128]{2,1,0:T(8,128)(2,1)} custom-call(bf16[64,3072]{1,0:T(8,128)(2,1)S(1)} %shard_map.147.weights, bf16[64,32,128]{2,1,0:T(8,128)(2,1)S(1)} %all-to-all-done.2.boxes, s32[1,16]{1,0:T(1,128)S(1)} %copy-done.13, s32[8,4]{1,0:T(8,128)S(1)} %copy.16.top_partners), custom_call_target="tpu_custom_call" | custom-call | flops 50331648 | bytes 524288 | tf_op jit(solution)/shard_map/pallas_call | solution.py:242
  85.0 7.4 %all-to-all-start.3 = ((bf16[8,64,128]{2,1,0:T(8,128)(2,1)}), bf16[8,64,128]{2,1,0:T(8,128)(2,1)S(1)}, u32[]{:S(2)}, u32[]{:S(2)}) async-start(bf16[8,64,128]{2,1,0:T(8,128)(2,1)} %shard_map.149), calls=%async_computation.3 | async-start | bytes 262144 | tf_op jit(solution)/shard_map/all_to_all | solution.py:249
  92.4 1.6 %copy-done = bf16[2,256,2048]{2,1,0:T(8,128)(2,1)S(1)} copy-done((bf16[2,256,2048]{2,1,0:T(8,128)(2,1)S(1)}, bf16[2,256,2048]{2,1,0:T(8,128)(2,1)}, u32[]{:S(2)}) %copy-start) | copy-done | bytes 2097176
  94.0 3.1 %shard_map.150.near = f32[2,256,512]{2,1,0:T(8,128)S(1)} custom-call(bf16[2,256,2048]{2,1,0:T(8,128)(2,1)S(1)} %copy-done, bf16[2,256,512]{2,1,0:T(8,128)(2,1)} %collective-permute-done.3.behind, bf16[2,256,512]{2,1,0:T(8,128)(2,1)S(1)} %copy-done.2, bf16[2,256,512]{2,1,0:T(8,128)(2,1)} %collective-permute-done.4.ahead, s32[2,8]{1,0:T(2,128)S(1)} %copy-done.12, ...), custom_call_target="tpu_custom_call" | custom-call | flops 1073741824 | bytes 4718592 | tf_op jit(solution)/shard_map/pallas_call | solution.py:254
  97.0 0.6 all-to-all-done.3.local
  97.7 1.1 %copy-done.4 = bf16[2,64,2560]{2,1,0:T(8,128)(2,1)S(1)} copy-done((bf16[2,64,2560]{2,1,0:T(8,128)(2,1)S(1)}, bf16[2,64,2560]{2,1,0:T(8,128)(2,1)}, u32[]{:S(2)}) %copy-start.4) | copy-done | bytes 655384
  98.8 5.0 %shard_map.151 = bf16[2,256,512]{2,1,0:T(8,128)(2,1)} custom-call(bf16[2,64,2560]{2,1,0:T(8,128)(2,1)S(1)} %copy-done.4, bf16[4,3,2,64,512]{4,3,2,1,0:T(8,128)(2,1)S(1)} %all_to_all.20.mine, bf16[4,3,2,64,512]{4,3,2,1,0:T(8,128)(2,1)} %collective-permute-done.2.other, s32[2,40]{1,0:T(2,128)S(1)} %copy-done.11, s32[2]{0:T(128)S(1)} %copy-done.14, ...), custom_call_target="tpu_custom_call" | custom-call | flops 335544320 | bytes 4718592 | tf_op jit(solution)/shard_map/pallas_call | solution.py:263
  (34 shorter events, 0.6 us)
Async XLA Ops:
  0.0 1.0 %copy-start.1 = (bf16[2,256,512]{2,1,0:T(8,128)(2,1)S(1)}, bf16[2,256,512]{2,1,0:T(8,128)(2,1)}, u32[]{:S(2)}) copy-start(bf16[2,256,512]{2,1,0:T(8,128)(2,1)} %own.1) | copy-start | bytes 1572868
  1.0 0.8 copy-start.6
  1.8 0.8 copy-start.10
  3.0 7.2 %collective-permute-start.1 = (bf16[2,64,512]{2,1,0:T(8,128)(2,1)S(1)}, bf16[2,64,512]{2,1,0:T(8,128)(2,1)S(1)}, u32[]{:S(2)}, u32[]{:S(2)}) collective-permute-start(bf16[2,64,512]{2,1,0:T(8,128)(2,1)S(1)} %get-tuple-element.7.own), channel_id=1, source_target_pairs={{8,0},{16,8},{24,16},{32,24},{40,32},{48,40},{56,48},{64,56},{72,6... | collective-permute-start | bytes 393224 | tf_op jit(solution)/shard_map/ppermute | solution.py:169
  4.3 7.4 %collective-permute-start = (bf16[2,64,512]{2,1,0:T(8,128)(2,1)S(1)}, bf16[2,64,512]{2,1,0:T(8,128)(2,1)S(1)}, u32[]{:S(2)}, u32[]{:S(2)}) collective-permute-start(bf16[2,64,512]{2,1,0:T(8,128)(2,1)S(1)} %get-tuple-element.7.own), channel_id=1, source_target_pairs={{0,8},{8,16},{16,24},{24,32},{32,40},{40,48},{48,56},{56,64},{64,7... | collective-permute-start | bytes 393224 | tf_op jit(solution)/shard_map/ppermute | solution.py:169
  31.4 35.8 %copy-start.2 = (bf16[2,256,512]{2,1,0:T(8,128)(2,1)S(1)}, bf16[2,256,512]{2,1,0:T(8,128)(2,1)}, u32[]{:S(2)}) copy-start(bf16[2,256,512]{2,1,0:T(8,128)(2,1)} %own.1) | copy-start | bytes 1572868
  31.4 40.9 %copy-start.16 = (s32[8,4]{0,1:T(4,128)S(1)}, s32[8,4]{0,1:T(4,128)}, u32[]{:S(2)}) copy-start(s32[8,4]{0,1:T(4,128)} %param.29) | copy-start | bytes 388
  31.4 41.0 %copy-start.5 = (bf16[8,64,256]{2,1,0:T(8,128)(2,1)S(1)}, bf16[8,64,256]{2,1,0:T(8,128)(2,1)}, u32[]{:S(2)}) copy-start(bf16[8,64,256]{2,1,0:T(8,128)(2,1)} %top_coupling.1) | copy-start | bytes 786436
  31.4 41.0 %copy-start.8 = (bf16[1,64,1024]{2,1,0:T(8,128)(2,1)S(1)}, bf16[1,64,1024]{2,1,0:T(8,128)(2,1)}, u32[]{:S(2)}) copy-start(bf16[1,64,1024]{2,1,0:T(8,128)(2,1)} %coupling.1) | copy-start | bytes 393220
  31.4 66.3 %collective-permute-start.2 = (bf16[4,3,2,64,512]{4,3,2,1,0:T(8,128)(2,1)S(1)}, bf16[4,3,2,64,512]{4,3,2,1,0:T(8,128)(2,1)}, u32[]{:S(2)}, u32[]{:S(2)}) collective-permute-start(bf16[4,3,2,64,512]{4,3,2,1,0:T(8,128)(2,1)S(1)} %all_to_all.20.mine), channel_id=1, source_target_pairs={{0,1},{1,0},{2,3},{3,2},{4,5},{5,4},{6,7},{7,6},{8,9},{9,8},{10,11... | collective-permute-start | bytes 4718600 | tf_op jit(solution)/shard_map/ppermute | solution.py:229
  47.6 35.8 %copy-start.13 = (s32[1,16]{1,0:T(1,128)S(1)}, s32[1,16]{1,0:T(1,128)}, u32[]{:S(2)}) copy-start(s32[1,16]{1,0:T(1,128)} %box_partners.1) | copy-start | bytes 196
  47.6 35.8 %all-to-all-start.2 = ((bf16[64,32,128]{2,1,0:T(8,128)(2,1)}), bf16[64,32,128]{2,1,0:T(8,128)(2,1)S(1)}, u32[]{:S(2)}, u32[]{:S(2)}) async-start(bf16[64,32,128]{2,1,0:T(8,128)(2,1)} %shard_map.148), calls=%async_computation.2 | async-start | bytes 1048576 | tf_op jit(solution)/shard_map/all_to_all | solution.py:219
  67.1 25.2 %collective-permute-start.3 = (bf16[2,256,512]{2,1,0:T(8,128)(2,1)S(1)}, bf16[2,256,512]{2,1,0:T(8,128)(2,1)}, u32[]{:S(2)}, u32[]{:S(2)}) collective-permute-start(bf16[2,256,512]{2,1,0:T(8,128)(2,1)S(1)} %copy-done.2), channel_id=1, source_target_pairs={{0,1},{1,2},{2,3},{3,4},{4,5},{5,6},{6,7},{7,8},{8,9},{9,10},{10,1... | collective-permute-start | bytes 1572872 | tf_op jit(solution)/shard_map/ppermute | solution.py:169
  70.3 22.1 %collective-permute-start.4 = (bf16[2,256,512]{2,1,0:T(8,128)(2,1)S(1)}, bf16[2,256,512]{2,1,0:T(8,128)(2,1)}, u32[]{:S(2)}, u32[]{:S(2)}) collective-permute-start(bf16[2,256,512]{2,1,0:T(8,128)(2,1)S(1)} %copy-done.2), channel_id=1, source_target_pairs={{1,0},{2,1},{3,2},{4,3},{5,4},{6,5},{7,6},{8,7},{9,8},{10,9},{11,1... | collective-permute-start | bytes 1572872 | tf_op jit(solution)/shard_map/ppermute | solution.py:169
  72.4 1.2 %copy-start.3 = (bf16[64,64,64]{2,1,0:T(8,128)(2,1)S(1)}, bf16[64,64,64]{2,1,0:T(8,128)(2,1)}, u32[]{:S(2)}) copy-start(bf16[64,64,64]{2,1,0:T(8,128)(2,1)} %transfer.4) | copy-start | bytes 1572868
  73.6 18.8 %copy-start.12 = (s32[2,8]{1,0:T(2,128)S(1)}, s32[2,8]{1,0:T(2,128)}, u32[]{:S(2)}) copy-start(s32[2,8]{1,0:T(2,128)} %leaves.1) | copy-start | bytes 196
  73.6 18.8 %copy-start.15 = (s32[2]{0:T(128)S(1)}, s32[2]{0:T(128)}, u32[]{:S(2)}) copy-start(s32[2]{0:T(128)} %count.1) | copy-start | bytes 28
  84.9 12.7 %copy-start.7 = (bf16[2,64,64]{2,1,0:T(8,128)(2,1)S(1)}, bf16[2,64,64]{2,1,0:T(8,128)(2,1)}, u32[]{:S(2)}) copy-start(bf16[2,64,64]{2,1,0:T(8,128)(2,1)} %transfer.5) | copy-start | bytes 49156
  85.0 12.7 %copy-start.9 = (bf16[2,64,256]{2,1,0:T(8,128)(2,1)S(1)}, bf16[2,64,256]{2,1,0:T(8,128)(2,1)}, u32[]{:S(2)}) copy-start(bf16[2,64,256]{2,1,0:T(8,128)(2,1)} %target.1) | copy-start | bytes 196612
  85.0 12.7 %copy-start.11 = (s32[2,40]{1,0:T(2,128)S(1)}, s32[2,40]{1,0:T(2,128)}, u32[]{:S(2)}) copy-start(s32[2,40]{1,0:T(2,128)} %far_leaves.1) | copy-start | bytes 964
  85.0 12.7 %copy-start.14 = (s32[2]{0:T(128)S(1)}, s32[2]{0:T(128)}, u32[]{:S(2)}) copy-start(s32[2]{0:T(128)} %far_count.1) | copy-start | bytes 28
  85.0 12.7 %all-to-all-start.3 = ((bf16[8,64,128]{2,1,0:T(8,128)(2,1)}), bf16[8,64,128]{2,1,0:T(8,128)(2,1)S(1)}, u32[]{:S(2)}, u32[]{:S(2)}) async-start(bf16[8,64,128]{2,1,0:T(8,128)(2,1)} %shard_map.149), calls=%async_computation.3 | async-start | bytes 262144 | tf_op jit(solution)/shard_map/all_to_all | solution.py:249
  92.4 1.6 %copy-start = (bf16[2,256,2048]{2,1,0:T(8,128)(2,1)S(1)}, bf16[2,256,2048]{2,1,0:T(8,128)(2,1)}, u32[]{:S(2)}) copy-start(bf16[2,256,2048]{2,1,0:T(8,128)(2,1)} %blocks.1) | copy-start | bytes 6291460
  97.7 1.1 %copy-start.4 = (bf16[2,64,2560]{2,1,0:T(8,128)(2,1)S(1)}, bf16[2,64,2560]{2,1,0:T(8,128)(2,1)}, u32[]{:S(2)}) copy-start(bf16[2,64,2560]{2,1,0:T(8,128)(2,1)} %far_coupling.1) | copy-start | bytes 1966084

commit v2 on v1

v2 whole, which is shorter than its diff:
```python
import functools

import jax
import jax.numpy as jnp
from jax import lax
from jax.experimental import pallas as pl
from jax.experimental.pallas import tpu as pltpu
from jax.sharding import Mesh, PartitionSpec as P

RANK = 64
CHILDREN = 8
F32 = jnp.float32
BF16 = jnp.bfloat16
VMEM = pltpu.VMEM
SMEM = pltpu.SMEM
HBM = pltpu.HBM
WIDE = 119 << 19


def dot(a, b):
    return jnp.dot(a, b, preferred_element_type=F32)


def dot_t(a, b):
    return lax.dot_general(a, b, (((0,), (0,)), ((), ())), preferred_element_type=F32)


def call(body, out_shape, spaces, flops, moved, scratch=(), limit=32 << 20, out_space=VMEM):
    outs = jax.tree.map(lambda _: pl.BlockSpec(memory_space=out_space), out_shape)
    return pl.pallas_call(
        body,
        out_shape=out_shape,
        in_specs=[pl.BlockSpec(memory_space=s) for s in spaces],
        out_specs=outs,
        scratch_shapes=list(scratch),
        compiler_params=pltpu.CompilerParams(vmem_limit_bytes=limit),
        cost_estimate=pl.CostEstimate(flops=flops, bytes_accessed=moved, transcendentals=0),
    )


def load_all(sources, places, sems):
    loads = [pltpu.make_async_copy(a, b, sems.at[i]) for i, (a, b) in enumerate(zip(sources, places))]
    for load in loads:
        load.start()
    return loads


def upward_body(groups, basis_far, densities_far, transfer_far, skeleton, pieces, basis, densities, transfer, sems):
    for load in load_all((basis_far, densities_far, transfer_far), (basis, densities, transfer), sems):
        load.wait()
    total = None
    for leaf in range(densities.shape[0]):
        value = dot(basis[leaf], densities[leaf]).astype(BF16)
        skeleton[leaf] = value
        term = dot(transfer[leaf], value)
        total = term if total is None else total + term
    total = total.astype(BF16)
    rows, cols = pieces.shape[1:]
    for piece in range(groups):
        top, left = (piece % 2) * rows, (piece // 2) * cols
        pieces[piece] = total[top : top + rows, left : left + cols]


def spread_body(arrived, even, own, odd, copies, joined):
    joined[0] = even[...]
    joined[1] = own[...]
    joined[2] = odd[...]
    total = arrived[0].astype(F32)
    for piece in range(1, arrived.shape[0]):
        total = total + arrived[piece].astype(F32)
    total = total.astype(BF16)
    for target in range(copies.shape[0]):
        copies[target] = total


def weight_body(coupling_far, transfer_far, top_far, top_partners, weights, coupling, own, row, transfer, sems):
    box = lax.axis_index("boxes")
    half = lax.axis_index("core")
    parent = box // CHILDREN
    slots = top_partners.shape[0]
    sources = [coupling_far.at[0], transfer_far.at[box], top_far.at[parent]]
    sources += [transfer_far.at[pl.ds(top_partners[slot, parent] * CHILDREN, CHILDREN)] for slot in range(slots)]
    loads = load_all(sources, [coupling, own, row] + [transfer.at[slot] for slot in range(slots)], sems)
    for load in loads:
        load.wait()
    lefts = dot_t(own[...], row[...])
    near = coupling.shape[-1]

    def keep(value):
        lane = lax.broadcasted_iota(jnp.int32, value.shape, 1)
        return jnp.where((lane // (RANK // 2)) % 2 == half, value, 0.0).astype(BF16)

    weights[:, :near] = keep(coupling[...].astype(F32))
    span = CHILDREN * RANK
    for slot in range(slots):
        left = lefts[:, slot * RANK : (slot + 1) * RANK].astype(BF16)
        wide = jnp.concatenate([dot(left, transfer[slot, k]) for k in range(CHILDREN)], axis=1)
        weights[:, near + slot * span : near + (slot + 1) * span] = keep(wide)


def box_body(weights, boxes, box_partners, top_partners, copies):
    parent = lax.axis_index("boxes") // CHILDREN
    sources = [box_partners[0, j] for j in range(box_partners.shape[1])]
    for slot in range(top_partners.shape[0]):
        first = top_partners[slot, parent] * CHILDREN
        sources += [first + k for k in range(CHILDREN)]
    total = None
    step = 4
    for at in range(0, len(sources), step):
        rows = []
        for source in sources[at : at + step]:
            value = boxes[source]
            rows += [value, value]
        term = dot(weights[:, at * RANK : (at + step) * RANK], jnp.concatenate(rows, axis=0))
        total = term if total is None else total + term
    total = total.astype(BF16)
    for target in range(copies.shape[0]):
        copies[target] = total


def place(offset, index):
    return jnp.where(index % 2 == 1, offset, 2 - offset)


def near_body(device_of, blocks, even, own, odd, leaves, count, out, window, sems):
    leaf_dev, points, _ = own.shape
    blank = 3 * leaf_dev
    places = [window.at[pl.ds(i * leaf_dev, leaf_dev)] for i in range(3)]
    loads = load_all((even, own, odd), places, sems)
    window[blank] = jnp.zeros(window.shape[1:], BF16)
    device = device_of()
    base = (device - 1) * leaf_dev
    for load in loads:
        load.wait()
    for leaf in range(leaf_dev):
        total = None
        for j in range(leaves.shape[1]):
            source = leaves[leaf, j] - base
            at = place(source // leaf_dev, device) * leaf_dev + source % leaf_dev
            value = window[jnp.where(j < count[leaf], at, blank)]
            term = dot(blocks[leaf, :, j * points : (j + 1) * points], value)
            total = term if total is None else total + term
        out[leaf] = total


def leaf_body(
    group_leaves,
    coupling_far,
    skeletons_far,
    near_far,
    transfer,
    target,
    far_leaves,
    far_count,
    local,
    out,
    coupling,
    skeletons,
    near,
    sems,
):
    box_of = lax.axis_index("boxes")
    leaf_dev = transfer.shape[0]
    blank = skeletons.shape[0] - 1
    loads = load_all(
        (coupling_far, skeletons_far, near_far), (coupling, skeletons.at[pl.ds(0, blank)], near), sems
    )
    skeletons[blank] = jnp.zeros(skeletons.shape[1:], BF16)
    parts = []
    for piece in range(0, local.shape[0], 2):
        parts.append(local[piece].astype(F32) + local[piece + 1].astype(F32))
    box_local = jnp.concatenate(parts, axis=1).astype(BF16)
    base = (box_of - 1) * group_leaves
    step = 4
    for load in loads[:2]:
        load.wait()
    for leaf in range(leaf_dev):
        total = dot_t(transfer[leaf], box_local)
        for at in range(0, far_leaves.shape[1], step):
            rows = []
            for j in range(at, at + step):
                source = far_leaves[leaf, j] - base
                within = source % group_leaves
                spot = place(source // group_leaves, box_of) * leaf_dev + within % leaf_dev
                spot = (within // leaf_dev) * 3 * leaf_dev + spot
                rows.append(skeletons[jnp.where(j < far_count[leaf], spot, blank)])
            total = total + dot(
                coupling[leaf, :, at * RANK : (at + step) * RANK], jnp.concatenate(rows, axis=0)
            )
        if leaf == 0:
            loads[2].wait()
        out[leaf] = (dot_t(target[leaf], total.astype(BF16)) + near[leaf]).astype(BF16)


def swap(block, axis, first):
    size = lax.axis_size(axis)
    pairs = [(i, i + 1) for i in range(first, size - 1, 2)]
    return lax.ppermute(block, axis, pairs + [(b, a) for a, b in pairs])


def shards(
    densities,
    basis_source,
    basis_target,
    near_blocks,
    near_leaves,
    near_count,
    far_coupling,
    far_leaves,
    far_count,
    leaf_transfer,
    box_transfer,
    box_coupling,
    box_partners,
    top_coupling,
    top_partners,
):
    chips, cores = lax.axis_size("x"), lax.axis_size("core")
    groups = chips * cores
    boxes = lax.axis_size("boxes")
    leaf_dev, points, vectors = densities.shape
    cols, rows = vectors // chips, RANK // cores
    grp = ("x", "core")
    line = ("boxes", "x", "core")

    skeleton, pieces = call(
        functools.partial(upward_body, groups),
        (
            jax.ShapeDtypeStruct((leaf_dev, RANK, vectors), BF16),
            jax.ShapeDtypeStruct((groups, rows, cols), BF16),
        ),
        [HBM] * 3,
        2 * leaf_dev * RANK * vectors * (points + RANK),
        densities.size * 2,
        (
            VMEM(basis_source.shape, BF16),
            VMEM(densities.shape, BF16),
            VMEM(leaf_transfer.shape, BF16),
            pltpu.SemaphoreType.DMA((3,)),
        ),
        WIDE,
    )(basis_source, densities, leaf_transfer)
    arrived = lax.all_to_all(pieces, grp, 0, 0, tiled=True)

    even_skeleton = swap(skeleton, "boxes", 0)
    odd_skeleton = swap(skeleton, "boxes", 1)

    spread, trio = call(
        spread_body,
        (
            jax.ShapeDtypeStruct((boxes, rows, cols), BF16),
            jax.ShapeDtypeStruct((3, leaf_dev, RANK, vectors), BF16),
        ),
        [VMEM] * 4,
        groups * rows * cols,
        boxes * rows * cols * 2,
    )(arrived, even_skeleton, skeleton, odd_skeleton)
    all_boxes = lax.all_to_all(spread, "boxes", 0, 0, tiled=True)
    window = lax.all_gather(trio, grp, axis=0, tiled=False)

    held, _ = lax.optimization_barrier((densities, spread))
    even = swap(held, line, 0)
    odd = swap(held, line, 1)

    tops = top_partners.T
    sources = box_partners.shape[1] + tops.shape[0] * CHILDREN
    weights = call(
        weight_body,
        jax.ShapeDtypeStruct((RANK, sources * RANK), BF16),
        [HBM, HBM, HBM, SMEM],
        2 * RANK * RANK * RANK * sources,
        box_transfer.size * 2,
        (
            VMEM(box_coupling.shape[1:], BF16),
            VMEM(box_transfer.shape[1:], BF16),
            VMEM(top_coupling.shape[1:], BF16),
            VMEM((tops.shape[0], CHILDREN) + box_transfer.shape[1:], BF16),
            pltpu.SemaphoreType.DMA((3 + tops.shape[0],)),
        ),
    )(box_coupling, box_transfer, top_coupling, tops)
    local = call(
        box_body,
        jax.ShapeDtypeStruct((groups, RANK, cols), BF16),
        [VMEM, VMEM, SMEM, SMEM],
        2 * RANK * RANK * sources * cols,
        all_boxes.size * 2,
    )(weights, all_boxes, box_partners, tops)
    local = lax.all_to_all(local, grp, 0, 0, tiled=True)

    def device_of():
        return (lax.axis_index("boxes") * chips + lax.axis_index("x")) * cores + lax.axis_index("core")

    near_field = call(
        functools.partial(near_body, device_of),
        jax.ShapeDtypeStruct((leaf_dev, points, vectors), F32),
        [VMEM] + [HBM] * 3 + [SMEM] * 2,
        2 * near_blocks.size * vectors,
        near_blocks.size * 2 + 5 * densities.size * 2,
        (
            VMEM((3 * leaf_dev + 1, points, vectors), BF16),
            pltpu.SemaphoreType.DMA((3,)),
        ),
    )(near_blocks, even, densities, odd, near_leaves, near_count)
    flat = window.reshape((groups * 3 * leaf_dev, RANK, vectors))
    return call(
        functools.partial(leaf_body, groups * leaf_dev),
        jax.ShapeDtypeStruct(densities.shape, BF16),
        [HBM] * 3 + [VMEM] * 2 + [SMEM] * 2 + [VMEM],
        2 * far_coupling.size * vectors,
        2 * window.size,
        (
            VMEM(far_coupling.shape, BF16),
            VMEM((flat.shape[0] + 1, RANK, vectors), BF16),
            VMEM(near_field.shape, F32),
            pltpu.SemaphoreType.DMA((3,)),
        ),
        WIDE,
    )(
        far_coupling,
        flat,
        near_field,
        leaf_transfer,
        basis_target,
        far_leaves,
        far_count,
        local,
    )


def solution(mesh):
    boxes, groups = mesh.devices.shape
    fine = Mesh(mesh.devices.reshape(boxes, groups // 2, 2), ("boxes", "x", "core"))
    line = ("boxes", "x", "core")
    leaf = P(line, None, None)
    placed = (
        leaf,
        leaf,
        leaf,
        leaf,
        P(line, None),
        P(line),
        leaf,
        P(line, None),
        P(line),
        leaf,
        P(),
        P("boxes", None, None),
        P("boxes", None),
        P(),
        P(),
    )
    return jax.shard_map(shards, mesh=fine, in_specs=placed, out_specs=leaf, check_vma=False)
```

time: 105 us -> 89.1 us (0.85)
  blocking collectives: 26.8 us -> 12.1 us
  between operations: 0.17 us -> 13.6 us
  starting transfers between devices: 46.9 us -> 33.9 us
  waiting for transfers between devices: 11.2 us -> 6.58 us
  Pallas kernels: 12.1 us -> 14.6 us
  local copies, waits for them, and re-layouts: 6.65 us -> 7.73 us
    all_to_all x1 -> x0, blocking collectives: 19.6 us -> none  [shards(): mine = lax.all_to_all(trio, 'x', 0, 0, tiled=True)]
    ppermute x5 -> x4, starting transfers between devices: 20 us -> 10.6 us  [swap(): return lax.ppermute(block, axis, pairs + [(b, a) for a, b in pairs])]
    all_to_all x1, blocking collectives: 7.23 us -> 12.1 us  [shards(): arrived = lax.all_to_all(pieces, grp, 0, 0, tiled=True)]
    all_to_all x1, waiting for transfers between devices: 8.67 us -> 5.31 us  [shards(): all_boxes = lax.all_to_all(spread, 'boxes', 0, 0, tiled=True)]
    all_to_all x1, starting transfers between devices: 19.5 us -> 16.1 us  [shards(): all_boxes = lax.all_to_all(spread, 'boxes', 0, 0, tiled=True)]
    ppermute x5 -> x4, waiting for transfers between devices: 1.93 us -> 0.01 us  [swap(): return lax.ppermute(block, axis, pairs + [(b, a) for a, b in pairs])]
    pallas_call x1, Pallas kernels: 0.36 us -> 2.23 us  [shards(): call(functools.partial(upward_body, groups), (jax.ShapeDtypeStruct((leaf_...]
    unnamed x35 -> x30, local copies, waits for them, and re-layouts: 6.65 us -> 7.73 us
  transfers between devices with their start and end apart: 7 -> 7, of which waited for: 4 -> 2; matrix products, arithmetic and copies ran while one was open for 0% -> 0% of each run, Pallas kernels for 6% -> 7%
where the time goes in v2:
time: 89.1 us; the launch traced here: 88.5 us
  starting transfers between devices  33.9 us (38%)
  Pallas kernels  14.6 us (16%)
  between operations  13.6 us (15%)
  blocking collectives  12.1 us (14%)
  local copies, waits for them, and re-layouts  7.73 us (9%)
  waiting for transfers between devices  6.58 us (7%)
    all_to_all x1, starting transfers between devices, shards(): all_boxes = lax.all_to_all(spread, 'boxes', 0, 0, tiled=True)  16.1 us
    all_to_all x1, blocking collectives, shards(): arrived = lax.all_to_all(pieces, grp, 0, 0, tiled=True)  12.1 us
    ppermute x4, starting transfers between devices, swap(): return lax.ppermute(block, axis, pairs + [(b, a) for a, b in pairs])  10.6 us
    unnamed x30, local copies, waits for them, and re-layouts  7.73 us
    all_to_all x1, starting transfers between devices, shards(): local = lax.all_to_all(local, grp, 0, 0, tiled=True)  7.23 us
    pallas_call x1, Pallas kernels, shards(): call(functools.partial(leaf_body, groups * leaf_dev), jax.ShapeDtypeStruc...  5.57 us
    all_to_all x1, waiting for transfers between devices, shards(): all_boxes = lax.all_to_all(spread, 'boxes', 0, 0, tiled=True)  5.31 us
    pallas_call x1, Pallas kernels, shards(): call(functools.partial(near_body, device_of), jax.ShapeDtypeStruct((leaf_...  3.04 us
  transfers between devices with their start and end apart: 7, of which 2 were waited for; matrix products, arithmetic and copies ran while one was open for 0% of the time, Pallas kernels for 7%

profile of v2, /device:TPU:1, one launch (start us, length us, event | category | flops | bytes accessed | tf_op | source)
XLA Modules:
  0.0 88.5 jit_solution(3391712238223794708)
XLA Ops:
  6.5 2.2 %shard_map.145 = (bf16[2,64,512]{2,1,0:T(8,128)(2,1)}, bf16[8,32,128]{2,1,0:T(8,128)(2,1)}) custom-call(bf16[2,64,256]{2,1,0:T(8,128)(2,1)} %basis_far.1, bf16[2,256,512]{2,1,0:T(8,128)(2,1)} %own.1, bf16[2,64,64]{2,1,0:T(8,128)(2,1)} %transfer.1), custom_call_target="tpu_custom_call" | custom-call | flops 41943040 | bytes 524288 | tf_op jit(solution)/shard_map/pallas_call | solution.py:226
  8.8 4.8 %collective-permute-start = (bf16[2,64,512]{2,1,0:T(8,128)(2,1)}, bf16[2,64,512]{2,1,0:T(8,128)(2,1)S(1)}, u32[]{:S(2)}, u32[]{:S(2)}) collective-permute-start(bf16[2,64,512]{2,1,0:T(8,128)(2,1)} %get-tuple-element.11.own), channel_id=1, source_target_pairs={{0,8},{16,24},{32,40},{48,56},{64,72},{80,88},{96,104},{112,120},{... | collective-permute-start | bytes 393224 | tf_op jit(solution)/shard_map/ppermute | solution.py:198
  13.6 0.7 collective-permute-start.1
  14.3 12.1 %all_to_all.15.arrived = bf16[8,32,128]{2,1,0:T(8,128)(2,1)S(1)} all-to-all(bf16[8,32,128]{2,1,0:T(8,128)(2,1)} %get-tuple-element.10), channel_id=1, replica_groups=mesh['boxes'=64,'x'=4,'core'=2] {'x','core'}, dimensions={0} | all-to-all | bytes 131072 | tf_op jit(solution)/shard_map/all_to_all | solution.py:243
  26.4 0.9 %copy-done.8 = bf16[2,64,512]{2,1,0:T(8,128)(2,1)S(1)} copy-done((bf16[2,64,512]{2,1,0:T(8,128)(2,1)S(1)}, bf16[2,64,512]{2,1,0:T(8,128)(2,1)}, u32[]{:S(2)}) %copy-start.8) | copy-done | bytes 131096
  27.3 0.8 shard_map.146
  28.1 0.8 copy-done.4
  28.9 16.1 %all-to-all-start.1 = ((bf16[64,32,128]{2,1,0:T(8,128)(2,1)}), bf16[64,32,128]{2,1,0:T(8,128)(2,1)S(1)}, u32[]{:S(2)}, u32[]{:S(2)}) async-start(bf16[64,32,128]{2,1,0:T(8,128)(2,1)} %copy-done.4), calls=%async_computation.1 | async-start | bytes 1048576 | tf_op jit(solution)/shard_map/all_to_all | solution.py:258
  45.0 3.0 %collective-permute-start.2 = (bf16[2,256,512]{2,1,0:T(8,128)(2,1)}, bf16[2,256,512]{2,1,0:T(8,128)(2,1)}, u32[]{:S(2)}, u32[]{:S(2)}) collective-permute-start(bf16[2,256,512]{2,1,0:T(8,128)(2,1)} %own.1), channel_id=1, source_target_pairs={{0,1},{2,3},{4,5},{6,7},{8,9},{10,11},{12,13},{14,15},{16,17},{18,... | collective-permute-start | bytes 1572872 | tf_op jit(solution)/shard_map/ppermute | solution.py:198
  48.0 2.1 %collective-permute-start.3 = (bf16[2,256,512]{2,1,0:T(8,128)(2,1)}, bf16[2,256,512]{2,1,0:T(8,128)(2,1)}, u32[]{:S(2)}, u32[]{:S(2)}) collective-permute-start(bf16[2,256,512]{2,1,0:T(8,128)(2,1)} %own.1), channel_id=1, source_target_pairs={{1,2},{3,4},{5,6},{7,8},{9,10},{11,12},{13,14},{15,16},{17,18},{19... | collective-permute-start | bytes 1572872 | tf_op jit(solution)/shard_map/ppermute | solution.py:198
  50.1 1.2 %copy-done.3 = bf16[64,64,64]{2,1,0:T(8,128)(2,1)S(1)} copy-done((bf16[64,64,64]{2,1,0:T(8,128)(2,1)S(1)}, bf16[64,64,64]{2,1,0:T(8,128)(2,1)}, u32[]{:S(2)}) %copy-start.3) | copy-done | bytes 524312
  51.4 0.9 %copy-done.6 = bf16[8,64,256]{2,1,0:T(8,128)(2,1)S(1)} copy-done((bf16[8,64,256]{2,1,0:T(8,128)(2,1)S(1)}, bf16[8,64,256]{2,1,0:T(8,128)(2,1)}, u32[]{:S(2)}) %copy-start.6) | copy-done | bytes 262168
  52.3 0.9 %copy-done.7 = bf16[1,64,1024]{2,1,0:T(8,128)(2,1)S(1)} copy-done((bf16[1,64,1024]{2,1,0:T(8,128)(2,1)S(1)}, bf16[1,64,1024]{2,1,0:T(8,128)(2,1)}, u32[]{:S(2)}) %copy-start.7) | copy-done | bytes 131096
  53.2 0.7 copy-done.9
  53.9 2.1 %shard_map.148.weights = bf16[64,3072]{1,0:T(8,128)(2,1)S(1)} custom-call(bf16[1,64,1024]{2,1,0:T(8,128)(2,1)S(1)} %copy-done.7, bf16[64,64,64]{2,1,0:T(8,128)(2,1)S(1)} %copy-done.3, bf16[8,64,256]{2,1,0:T(8,128)(2,1)S(1)} %copy-done.6, s32[4,8]{1,0:T(4,128)S(1)} %bitcast.2), custom_call_target="tpu_custom_call" | custom-call | flops 25165824 | bytes 524288 | tf_op jit(solution)/shard_map/pallas_call | solution.py:267
  56.0 5.3 %all-to-all-done.1.boxes = bf16[64,32,128]{2,1,0:T(8,128)(2,1)S(1)} async-done(((bf16[64,32,128]{2,1,0:T(8,128)(2,1)}), bf16[64,32,128]{2,1,0:T(8,128)(2,1)S(1)}, u32[]{:S(2)}, u32[]{:S(2)}) %all-to-all-start.1) | async-done | bytes 524320 | tf_op jit(solution)/shard_map/all_to_all | solution.py:258
  61.3 0.8 shard_map.149
  62.2 0.6 copy-done.5
  62.8 7.2 %all-to-all-start.2 = ((bf16[8,64,128]{2,1,0:T(8,128)(2,1)}), bf16[8,64,128]{2,1,0:T(8,128)(2,1)S(1)}, u32[]{:S(2)}, u32[]{:S(2)}) async-start(bf16[8,64,128]{2,1,0:T(8,128)(2,1)} %copy-done.5), calls=%async_computation.2 | async-start | bytes 262144 | tf_op jit(solution)/shard_map/all_to_all | solution.py:288
  70.1 3.0 %shard_map.147.near_far = f32[2,256,512]{2,1,0:T(8,128)S(1)} custom-call(bf16[2,256,2048]{2,1,0:T(8,128)(2,1)S(1)} %copy-done.1, bf16[2,256,512]{2,1,0:T(8,128)(2,1)} %collective-permute-done.2.even, bf16[2,256,512]{2,1,0:T(8,128)(2,1)S(1)} %copy-done.2, bf16[2,256,512]{2,1,0:T(8,128)(2,1)} %collective-permute-done.3.odd, s32[2,8]{1,0:T(2,128)S(1)} %copy-done.11, ...), custom_call_target="tpu_custom_call" | custom-call | flops 1073741824 | bytes 4718592 | tf_op jit(solution)/shard_map/pallas_call | solution.py:293
  73.2 0.9 %copy-done = f32[2,256,512]{2,1,0:T(8,128)} copy-done((f32[2,256,512]{2,1,0:T(8,128)}, f32[2,256,512]{2,1,0:T(8,128)S(1)}, u32[]{:S(2)}) %copy-start) | copy-done | bytes 1048600
  74.1 1.2 %all-to-all-done.2.local = bf16[8,64,128]{2,1,0:T(8,128)(2,1)S(1)} async-done(((bf16[8,64,128]{2,1,0:T(8,128)(2,1)}), bf16[8,64,128]{2,1,0:T(8,128)(2,1)S(1)}, u32[]{:S(2)}, u32[]{:S(2)}) %all-to-all-start.2) | async-done | bytes 131104 | tf_op jit(solution)/shard_map/all_to_all | solution.py:288
  75.4 0.6 copy-done.14
  76.0 5.6 %shard_map.150 = bf16[2,256,512]{2,1,0:T(8,128)(2,1)} custom-call(bf16[2,64,2560]{2,1,0:T(8,128)(2,1)} %coupling_far.3, bf16[48,64,512]{2,1,0:T(8,128)(2,1)} %bitcast.4, f32[2,256,512]{2,1,0:T(8,128)} %copy-done, bf16[2,64,64]{2,1,0:T(8,128)(2,1)} %transfer.1, bf16[2,64,256]{2,1,0:T(8,128)(2,1)} %target.1, s32[2,40]{1,0:T(2,128)} %far_leaves.1, s32[2]{0:T(128)} %far_count.1, ...), custom_call_target="tpu_custom_call" | custom-call | flops 335544320 | bytes 3145728 | tf_op jit(solution)/shard_map/pallas_call | solution.py:305
  (28 shorter events, 0.1 us)
Async XLA Ops:
  6.5 63.6 %copy-start.2 = (bf16[2,256,512]{2,1,0:T(8,128)(2,1)S(1)}, bf16[2,256,512]{2,1,0:T(8,128)(2,1)}, u32[]{:S(2)}) copy-start(bf16[2,256,512]{2,1,0:T(8,128)(2,1)} %own.1) | copy-start | bytes 1572868
  6.5 63.6 %copy-start.1 = (bf16[2,256,2048]{2,1,0:T(8,128)(2,1)S(1)}, bf16[2,256,2048]{2,1,0:T(8,128)(2,1)}, u32[]{:S(2)}) copy-start(bf16[2,256,2048]{2,1,0:T(8,128)(2,1)} %blocks.1) | copy-start | bytes 6291460
  6.5 68.8 %all-gather.3.cloned.1.call-start = ((), (), s32[]{:S(2)}) async-start(), calls=%async_computation.3 | async-start | bytes 3538944 | tf_op jit(solution)/shard_map/all_gather | solution.py:259
  8.8 17.6 %collective-permute-start = (bf16[2,64,512]{2,1,0:T(8,128)(2,1)}, bf16[2,64,512]{2,1,0:T(8,128)(2,1)S(1)}, u32[]{:S(2)}, u32[]{:S(2)}) collective-permute-start(bf16[2,64,512]{2,1,0:T(8,128)(2,1)} %get-tuple-element.11.own), channel_id=1, source_target_pairs={{0,8},{16,24},{32,40},{48,56},{64,72},{80,88},{96,104},{112,120},{... | collective-permute-start | bytes 393224 | tf_op jit(solution)/shard_map/ppermute | solution.py:198
  13.6 12.8 %collective-permute-start.1 = (bf16[2,64,512]{2,1,0:T(8,128)(2,1)}, bf16[2,64,512]{2,1,0:T(8,128)(2,1)S(1)}, u32[]{:S(2)}, u32[]{:S(2)}) collective-permute-start(bf16[2,64,512]{2,1,0:T(8,128)(2,1)} %get-tuple-element.11.own), channel_id=1, source_target_pairs={{8,16},{24,32},{40,48},{56,64},{72,80},{88,96},{104,112},{120,128}... | collective-permute-start | bytes 393224 | tf_op jit(solution)/shard_map/ppermute | solution.py:198
  26.4 0.9 %copy-start.8 = (bf16[2,64,512]{2,1,0:T(8,128)(2,1)S(1)}, bf16[2,64,512]{2,1,0:T(8,128)(2,1)}, u32[]{:S(2)}) copy-start(bf16[2,64,512]{2,1,0:T(8,128)(2,1)} %get-tuple-element.11.own) | copy-start | bytes 393220
  27.3 34.1 %copy-start.10 = (s32[8,4]{0,1:T(4,128)S(1)}, s32[8,4]{0,1:T(4,128)}, u32[]{:S(2)}) copy-start(s32[8,4]{0,1:T(4,128)} %param.29) | copy-start | bytes 388
  27.3 34.1 %copy-start.12 = (s32[1,16]{1,0:T(1,128)S(1)}, s32[1,16]{1,0:T(1,128)}, u32[]{:S(2)}) copy-start(s32[1,16]{1,0:T(1,128)} %box_partners.1) | copy-start | bytes 196
  27.3 42.8 %copy-start.11 = (s32[2,8]{1,0:T(2,128)S(1)}, s32[2,8]{1,0:T(2,128)}, u32[]{:S(2)}) copy-start(s32[2,8]{1,0:T(2,128)} %leaves.1) | copy-start | bytes 196
  27.3 42.8 %copy-start.13 = (s32[2]{0:T(128)S(1)}, s32[2]{0:T(128)}, u32[]{:S(2)}) copy-start(s32[2]{0:T(128)} %count.1) | copy-start | bytes 28
  28.1 0.8 copy-start.4
  28.9 32.4 %all-to-all-start.1 = ((bf16[64,32,128]{2,1,0:T(8,128)(2,1)}), bf16[64,32,128]{2,1,0:T(8,128)(2,1)S(1)}, u32[]{:S(2)}, u32[]{:S(2)}) async-start(bf16[64,32,128]{2,1,0:T(8,128)(2,1)} %copy-done.4), calls=%async_computation.1 | async-start | bytes 1048576 | tf_op jit(solution)/shard_map/all_to_all | solution.py:258
  45.0 25.0 %collective-permute-start.2 = (bf16[2,256,512]{2,1,0:T(8,128)(2,1)}, bf16[2,256,512]{2,1,0:T(8,128)(2,1)}, u32[]{:S(2)}, u32[]{:S(2)}) collective-permute-start(bf16[2,256,512]{2,1,0:T(8,128)(2,1)} %own.1), channel_id=1, source_target_pairs={{0,1},{2,3},{4,5},{6,7},{8,9},{10,11},{12,13},{14,15},{16,17},{18,... | collective-permute-start | bytes 1572872 | tf_op jit(solution)/shard_map/ppermute | solution.py:198
  48.0 22.1 %collective-permute-start.3 = (bf16[2,256,512]{2,1,0:T(8,128)(2,1)}, bf16[2,256,512]{2,1,0:T(8,128)(2,1)}, u32[]{:S(2)}, u32[]{:S(2)}) collective-permute-start(bf16[2,256,512]{2,1,0:T(8,128)(2,1)} %own.1), channel_id=1, source_target_pairs={{1,2},{3,4},{5,6},{7,8},{9,10},{11,12},{13,14},{15,16},{17,18},{19... | collective-permute-start | bytes 1572872 | tf_op jit(solution)/shard_map/ppermute | solution.py:198
  50.1 1.2 %copy-start.3 = (bf16[64,64,64]{2,1,0:T(8,128)(2,1)S(1)}, bf16[64,64,64]{2,1,0:T(8,128)(2,1)}, u32[]{:S(2)}) copy-start(bf16[64,64,64]{2,1,0:T(8,128)(2,1)} %transfer_far.3) | copy-start | bytes 1572868
  51.4 0.9 %copy-start.6 = (bf16[8,64,256]{2,1,0:T(8,128)(2,1)S(1)}, bf16[8,64,256]{2,1,0:T(8,128)(2,1)}, u32[]{:S(2)}) copy-start(bf16[8,64,256]{2,1,0:T(8,128)(2,1)} %top_far.1) | copy-start | bytes 786436
  52.3 0.9 %copy-start.7 = (bf16[1,64,1024]{2,1,0:T(8,128)(2,1)S(1)}, bf16[1,64,1024]{2,1,0:T(8,128)(2,1)}, u32[]{:S(2)}) copy-start(bf16[1,64,1024]{2,1,0:T(8,128)(2,1)} %coupling_far.2) | copy-start | bytes 393220
  53.2 0.7 copy-start.9
  62.2 0.7 copy-start.5
  62.8 12.5 %all-to-all-start.2 = ((bf16[8,64,128]{2,1,0:T(8,128)(2,1)}), bf16[8,64,128]{2,1,0:T(8,128)(2,1)S(1)}, u32[]{:S(2)}, u32[]{:S(2)}) async-start(bf16[8,64,128]{2,1,0:T(8,128)(2,1)} %copy-done.5), calls=%async_computation.2 | async-start | bytes 262144 | tf_op jit(solution)/shard_map/all_to_all | solution.py:288
  73.2 1.0 %copy-start = (f32[2,256,512]{2,1,0:T(8,128)}, f32[2,256,512]{2,1,0:T(8,128)S(1)}, u32[]{:S(2)}) copy-start(f32[2,256,512]{2,1,0:T(8,128)S(1)} %shard_map.147.near_far) | copy-start | bytes 3145732
  75.4 0.7 copy-start.14
Sparse Core Ops, SparseCore 0:
  29.0 39.7 all-gather.2

commit v3 on v2

--- a/solution.py
+++ b/solution.py
@@ -15,6 +15,7 @@
 SMEM = pltpu.SMEM
 HBM = pltpu.HBM
 WIDE = 119 << 19
+HUGE = 10**9
 
 
 def dot(a, b):
@@ -61,7 +62,18 @@
         pieces[piece] = total[top : top + rows, left : left + cols]
 
 
-def spread_body(arrived, even, own, odd, copies, joined):
+def pair_body(first, second, joined):
+    joined[0] = first[...]
+    joined[1] = second[...]
+
+
+def join_body(first, second, after, even, odd, joined):
+    half = first.shape[0]
+    joined[:half] = first[...]
+    joined[half:] = second[...]
+
+
+def spread_body(arrived, even, own, odd, before, copies, joined):
     joined[0] = even[...]
     joined[1] = own[...]
     joined[2] = odd[...]
@@ -122,17 +134,22 @@
     return jnp.where(index % 2 == 1, offset, 2 - offset)
 
 
-def near_body(device_of, blocks, even, own, odd, leaves, count, out, window, sems):
+def near_body(
+    device_of, blocks_far, even, own, odd, leaves_far, count_far, out_far, blocks, window, leaves, count, out, sems, out_sems
+):
     leaf_dev, points, _ = own.shape
     blank = 3 * leaf_dev
-    places = [window.at[pl.ds(i * leaf_dev, leaf_dev)] for i in range(3)]
-    loads = load_all((even, own, odd), places, sems)
+    sources = [leaves_far, count_far, even, own, odd] + [blocks_far.at[leaf] for leaf in range(leaf_dev)]
+    places = [leaves, count] + [window.at[pl.ds(i * leaf_dev, leaf_dev)] for i in range(3)]
+    loads = load_all(sources, places + [blocks.at[leaf] for leaf in range(leaf_dev)], sems)
     window[blank] = jnp.zeros(window.shape[1:], BF16)
     device = device_of()
     base = (device - 1) * leaf_dev
-    for load in loads:
+    for load in loads[:5]:
         load.wait()
+    stores = []
     for leaf in range(leaf_dev):
+        loads[5 + leaf].wait()
         total = None
         for j in range(leaves.shape[1]):
             source = leaves[leaf, j] - base
@@ -141,39 +158,67 @@
             term = dot(blocks[leaf, :, j * points : (j + 1) * points], value)
             total = term if total is None else total + term
         out[leaf] = total
+        stores += load_all((out.at[leaf],), (out_far.at[leaf],), out_sems.at[pl.ds(leaf, 1)])
+    for store in stores:
+        store.wait()
 
 
 def leaf_body(
     group_leaves,
     coupling_far,
-    skeletons_far,
+    mine,
+    other,
     near_far,
+    transfer_far,
+    target_far,
+    far_leaves_far,
+    far_count_far,
+    local_far,
+    out_far,
+    coupling,
+    skeletons,
+    near,
     transfer,
     target,
     far_leaves,
     far_count,
     local,
     out,
-    coupling,
-    skeletons,
-    near,
     sems,
+    out_sems,
 ):
     box_of = lax.axis_index("boxes")
     leaf_dev = transfer.shape[0]
     blank = skeletons.shape[0] - 1
+    half = lax.axis_index("core")
+    chip_of = lax.axis_index("x")
     loads = load_all(
-        (coupling_far, skeletons_far, near_far), (coupling, skeletons.at[pl.ds(0, blank)], near), sems
+        (far_leaves_far, far_count_far, local_far, transfer_far, coupling_far, mine, other, target_far, near_far),
+        (
+            far_leaves,
+            far_count,
+            local,
+            transfer,
+            coupling,
+            skeletons.at[pl.ds(half * (blank // 2), blank // 2)],
+            skeletons.at[pl.ds((1 - half) * (blank // 2), blank // 2)],
+            target,
+            near,
+        ),
+        sems,
     )
     skeletons[blank] = jnp.zeros(skeletons.shape[1:], BF16)
+    for load in loads[:3]:
+        load.wait()
     parts = []
     for piece in range(0, local.shape[0], 2):
         parts.append(local[piece].astype(F32) + local[piece + 1].astype(F32))
     box_local = jnp.concatenate(parts, axis=1).astype(BF16)
     base = (box_of - 1) * group_leaves
     step = 4
-    for load in loads[:2]:
+    for load in loads[3:7]:
         load.wait()
+    stores = []
     for leaf in range(leaf_dev):
         total = dot_t(transfer[leaf], box_local)
         for at in range(0, far_leaves.shape[1], step):
@@ -182,14 +227,20 @@
                 source = far_leaves[leaf, j] - base
                 within = source % group_leaves
                 spot = place(source // group_leaves, box_of) * leaf_dev + within % leaf_dev
-                spot = (within // leaf_dev) * 3 * leaf_dev + spot
+                side, chip = (within // leaf_dev) % 2, (within // (2 * leaf_dev)) ^ chip_of
+                chip = chip ^ (chip // 2)
+                spot = side * (blank // 2) + chip * 3 * leaf_dev + spot
                 rows.append(skeletons[jnp.where(j < far_count[leaf], spot, blank)])
             total = total + dot(
                 coupling[leaf, :, at * RANK : (at + step) * RANK], jnp.concatenate(rows, axis=0)
             )
         if leaf == 0:
-            loads[2].wait()
+            for load in loads[7:]:
+                load.wait()
         out[leaf] = (dot_t(target[leaf], total.astype(BF16)) + near[leaf]).astype(BF16)
+        stores += load_all((out.at[leaf],), (out_far.at[leaf],), out_sems.at[pl.ds(leaf, 1)])
+    for store in stores:
+        store.wait()
 
 
 def swap(block, axis, first):
@@ -245,23 +296,6 @@
     even_skeleton = swap(skeleton, "boxes", 0)
     odd_skeleton = swap(skeleton, "boxes", 1)
 
-    spread, trio = call(
-        spread_body,
-        (
-            jax.ShapeDtypeStruct((boxes, rows, cols), BF16),
-            jax.ShapeDtypeStruct((3, leaf_dev, RANK, vectors), BF16),
-        ),
-        [VMEM] * 4,
-        groups * rows * cols,
-        boxes * rows * cols * 2,
-    )(arrived, even_skeleton, skeleton, odd_skeleton)
-    all_boxes = lax.all_to_all(spread, "boxes", 0, 0, tiled=True)
-    window = lax.all_gather(trio, grp, axis=0, tiled=False)
-
-    held, _ = lax.optimization_barrier((densities, spread))
-    even = swap(held, line, 0)
-    odd = swap(held, line, 1)
-
     tops = top_partners.T
     sources = box_partners.shape[1] + tops.shape[0] * CHILDREN
     weights = call(
@@ -277,7 +311,33 @@
             VMEM((tops.shape[0], CHILDREN) + box_transfer.shape[1:], BF16),
             pltpu.SemaphoreType.DMA((3 + tops.shape[0],)),
         ),
+        WIDE,
     )(box_coupling, box_transfer, top_coupling, tops)
+    spread, trio = call(
+        spread_body,
+        (
+            jax.ShapeDtypeStruct((boxes, rows, cols), BF16),
+            jax.ShapeDtypeStruct((3, leaf_dev, RANK, vectors), BF16),
+        ),
+        [VMEM] * 4 + [pl.ANY],
+        groups * rows * cols,
+        boxes * rows * cols * 2,
+    )(arrived, even_skeleton, skeleton, odd_skeleton, weights)
+    all_boxes = lax.all_to_all(spread, "boxes", 0, 0, tiled=True)
+    flips = [[(i, i ^ flip) for i in range(chips)] for flip in (1, 3)]
+    pair = call(
+        pair_body,
+        jax.ShapeDtypeStruct((2,) + trio.shape, BF16),
+        [VMEM] * 2,
+        HUGE,
+        4 * trio.size * 2,
+    )(trio, lax.ppermute(trio, "x", flips[0]))
+    opposite = lax.ppermute(pair, "x", flips[1])
+
+    held, _ = lax.optimization_barrier((densities, pair))
+    even = swap(held, line, 0)
+    odd = swap(held, line, 1)
+
     local = call(
         box_body,
         jax.ShapeDtypeStruct((groups, RANK, cols), BF16),
@@ -286,6 +346,14 @@
         all_boxes.size * 2,
     )(weights, all_boxes, box_partners, tops)
     local = lax.all_to_all(local, grp, 0, 0, tiled=True)
+    mine = call(
+        join_body,
+        jax.ShapeDtypeStruct((chips,) + trio.shape, BF16),
+        [VMEM] * 2 + [pl.ANY] * 3,
+        0,
+        2 * chips * trio.size * 2,
+    )(pair, opposite, local, even, odd)
+    other = swap(mine, "core", 0)
 
     def device_of():
         return (lax.axis_index("boxes") * chips + lax.axis_index("x")) * cores + lax.axis_index("core")
@@ -293,31 +361,47 @@
     near_field = call(
         functools.partial(near_body, device_of),
         jax.ShapeDtypeStruct((leaf_dev, points, vectors), F32),
-        [VMEM] + [HBM] * 3 + [SMEM] * 2,
+        [HBM] + [pl.ANY] * 5,
         2 * near_blocks.size * vectors,
         near_blocks.size * 2 + 5 * densities.size * 2,
         (
+            VMEM(near_blocks.shape, BF16),
             VMEM((3 * leaf_dev + 1, points, vectors), BF16),
-            pltpu.SemaphoreType.DMA((3,)),
-        ),
+            SMEM(near_leaves.shape, jnp.int32),
+            SMEM(near_count.shape, jnp.int32),
+            VMEM((leaf_dev, points, vectors), F32),
+            pltpu.SemaphoreType.DMA((5 + leaf_dev,)),
+            pltpu.SemaphoreType.DMA((leaf_dev,)),
+        ),
+        32 << 20,
+        HBM,
     )(near_blocks, even, densities, odd, near_leaves, near_count)
-    flat = window.reshape((groups * 3 * leaf_dev, RANK, vectors))
+    flat = (chips * 3 * leaf_dev, RANK, vectors)
     return call(
         functools.partial(leaf_body, groups * leaf_dev),
         jax.ShapeDtypeStruct(densities.shape, BF16),
-        [HBM] * 3 + [VMEM] * 2 + [SMEM] * 2 + [VMEM],
+        [HBM] * 4 + [pl.ANY] * 5,
         2 * far_coupling.size * vectors,
-        2 * window.size,
+        4 * mine.size,
         (
             VMEM(far_coupling.shape, BF16),
-            VMEM((flat.shape[0] + 1, RANK, vectors), BF16),
+            VMEM((cores * flat[0] + 1, RANK, vectors), BF16),
             VMEM(near_field.shape, F32),
-            pltpu.SemaphoreType.DMA((3,)),
-        ),
-        WIDE,
+            VMEM(leaf_transfer.shape, BF16),
+            VMEM(basis_target.shape, BF16),
+            SMEM(far_leaves.shape, jnp.int32),
+            SMEM(far_count.shape, jnp.int32),
+            VMEM(local.shape, BF16),
+            VMEM(densities.shape, BF16),
+            pltpu.SemaphoreType.DMA((9,)),
+            pltpu.SemaphoreType.DMA((leaf_dev,)),
+        ),
+        32 << 20,
+        HBM,
     )(
         far_coupling,
-        flat,
+        mine.reshape(flat),
+        other.reshape(flat),
         near_field,
         leaf_transfer,
         basis_target,

time: 89.1 us -> 82.8 us (0.929)
  starting transfers between devices: 33.9 us -> 50.3 us
  between operations: 13.6 us -> 0.25 us
  blocking collectives: 12.1 us -> 0 us
  waiting for transfers between devices: 6.58 us -> 13.5 us
  local copies, waits for them, and re-layouts: 7.73 us -> 1.05 us
  Pallas kernels: 14.6 us -> 16.9 us
    all_to_all x1 -> x0, blocking collectives: 12.1 us -> none  [shards(): arrived = lax.all_to_all(pieces, grp, 0, 0, tiled=True)]
    ppermute x4 -> x5, starting transfers between devices: 10.6 us -> 17.3 us  [swap(): return lax.ppermute(block, axis, pairs + [(b, a) for a, b in pairs])]
    unnamed x30 -> x26, local copies, waits for them, and re-layouts: 7.73 us -> 1.05 us
    all_to_all x0 -> x1, starting transfers between devices: none -> 5.55 us  [shards(): arrived = lax.all_to_all(pieces, grp, 0, 0, tiled=True)]
    ppermute x0 -> x2, starting transfers between devices: none -> 5.45 us  [the longest x1 3.27 us: shards(): opposite = lax.ppermute(pair, 'x', flips[1])]
    all_to_all x1, waiting for transfers between devices: 1.24 us -> 5.24 us  [shards(): local = lax.all_to_all(local, grp, 0, 0, tiled=True)]
    pallas_call x0 -> x2, Pallas kernels: none -> 2.41 us  [the longest x1 1.47 us: shards(): call(join_body, jax.ShapeDtypeStruct((chips,) + trio.shape, BF16), [VMEM]...]
    all_to_all x1, starting transfers between devices: 16.1 us -> 14.5 us  [shards(): all_boxes = lax.all_to_all(spread, 'boxes', 0, 0, tiled=True)]
  transfers between devices with their start and end apart: 7 -> 10, of which waited for: 2 -> 4; matrix products, arithmetic and copies ran while one was open for 0% -> 0% of each run, Pallas kernels for 7% -> 10%
where the time goes in v3:
time: 82.8 us; the launch traced here: 82.1 us
  starting transfers between devices  50.3 us (61%)
  Pallas kernels  16.9 us (20%)
  waiting for transfers between devices  13.5 us (16%)
  local copies, waits for them, and re-layouts  1.05 us (1%)
    ppermute x5, starting transfers between devices, swap(): return lax.ppermute(block, axis, pairs + [(b, a) for a, b in pairs])  17.3 us
    all_to_all x1, starting transfers between devices, shards(): all_boxes = lax.all_to_all(spread, 'boxes', 0, 0, tiled=True)  14.5 us
    all_to_all x1, starting transfers between devices, shards(): local = lax.all_to_all(local, grp, 0, 0, tiled=True)  7.55 us
    all_to_all x1, waiting for transfers between devices, shards(): all_boxes = lax.all_to_all(spread, 'boxes', 0, 0, tiled=True)  6.43 us
    all_to_all x1, starting transfers between devices, shards(): arrived = lax.all_to_all(pieces, grp, 0, 0, tiled=True)  5.55 us
    all_to_all x1, waiting for transfers between devices, shards(): local = lax.all_to_all(local, grp, 0, 0, tiled=True)  5.24 us
    pallas_call x1, Pallas kernels, shards(): call(functools.partial(leaf_body, groups * leaf_dev), jax.ShapeDtypeStruc...  4.07 us
    pallas_call x1, Pallas kernels, shards(): call(weight_body, jax.ShapeDtypeStruct((RANK, sources * RANK), BF16), [HB...  3.29 us
  transfers between devices with their start and end apart: 10, of which 4 were waited for; matrix products, arithmetic and copies ran while one was open for 0% of the time, Pallas kernels for 10%

profile of v3, /device:TPU:1, one launch (start us, length us, event | category | flops | bytes accessed | tf_op | source)
XLA Modules:
  0.0 82.1 jit_solution(15980590153770676963)
XLA Ops:
  0.0 2.1 %shard_map.145 = (bf16[2,64,512]{2,1,0:T(8,128)(2,1)}, bf16[8,32,128]{2,1,0:T(8,128)(2,1)}) custom-call(bf16[2,64,256]{2,1,0:T(8,128)(2,1)} %basis_far.1, bf16[2,256,512]{2,1,0:T(8,128)(2,1)} %own.1, bf16[2,64,64]{2,1,0:T(8,128)(2,1)} %transfer_far.5), custom_call_target="tpu_custom_call" | custom-call | flops 41943040 | bytes 524288 | tf_op jit(solution)/shard_map/pallas_call | solution.py:277
  2.1 0.0 copy-start.5
  2.1 0.8 collective-permute-start.1
  2.9 8.2 %collective-permute-start = (bf16[2,64,512]{2,1,0:T(8,128)(2,1)}, bf16[2,64,512]{2,1,0:T(8,128)(2,1)S(1)}, u32[]{:S(2)}, u32[]{:S(2)}) collective-permute-start(bf16[2,64,512]{2,1,0:T(8,128)(2,1)} %get-tuple-element.11.own), channel_id=1, source_target_pairs={{0,8},{16,24},{32,40},{48,56},{64,72},{80,88},{96,104},{112,120},{... | collective-permute-start | bytes 393224 | tf_op jit(solution)/shard_map/ppermute | solution.py:249
  11.1 5.5 %all-to-all-start = ((bf16[8,32,128]{2,1,0:T(8,128)(2,1)}), bf16[8,32,128]{2,1,0:T(8,128)(2,1)S(1)}, u32[]{:S(2)}, u32[]{:S(2)}) async-start(bf16[8,32,128]{2,1,0:T(8,128)(2,1)} %get-tuple-element.10), calls=%async_computation | async-start | bytes 131072 | tf_op jit(solution)/shard_map/all_to_all | solution.py:294
  16.6 3.3 %shard_map.146.before.weights = bf16[64,3072]{1,0:T(8,128)(2,1)} custom-call(bf16[1,64,1024]{2,1,0:T(8,128)(2,1)} %coupling_far.2, bf16[64,64,64]{2,1,0:T(8,128)(2,1)} %transfer_far.4, bf16[8,64,256]{2,1,0:T(8,128)(2,1)} %top_far.1, s32[4,8]{1,0:T(4,128)} %bitcast.5), custom_call_target="tpu_custom_call" | custom-call | flops 25165824 | bytes 524288 | tf_op jit(solution)/shard_map/pallas_call | solution.py:301
  19.9 1.5 %all-to-all-done.arrived = bf16[8,32,128]{2,1,0:T(8,128)(2,1)S(1)} async-done(((bf16[8,32,128]{2,1,0:T(8,128)(2,1)}), bf16[8,32,128]{2,1,0:T(8,128)(2,1)S(1)}, u32[]{:S(2)}, u32[]{:S(2)}) %all-to-all-start) | async-done | bytes 65568 | tf_op jit(solution)/shard_map/all_to_all | solution.py:294
  21.5 1.0 %copy-done = bf16[64,3072]{1,0:T(8,128)(2,1)S(1)} copy-done((bf16[64,3072]{1,0:T(8,128)(2,1)S(1)}, bf16[64,3072]{1,0:T(8,128)(2,1)}, u32[]{:S(2)}) %copy-start) | copy-done | bytes 393240
  22.5 0.9 %shard_map.147 = (bf16[64,32,128]{2,1,0:T(8,128)(2,1)}, bf16[3,2,64,512]{3,2,1,0:T(8,128)(2,1)S(1)}) custom-call(bf16[8,32,128]{2,1,0:T(8,128)(2,1)S(1)} %all-to-all-done.arrived, bf16[2,64,512]{2,1,0:T(8,128)(2,1)S(1)} %collective-permute-done.even, bf16[2,64,512]{2,1,0:T(8,128)(2,1)S(1)} %copy-done.5, bf16[2,64,512]{2,1,0:T(8,128)(2,1)S(1)} %collective-permute-done.1.odd, ...), custom_call_target="tpu_custom_call" | custom-call | flops 32768 | bytes 524288 | tf_op jit(solution)/shard_map/pallas_call | solution.py:316
  23.3 2.2 %collective-permute-start.2 = (bf16[3,2,64,512]{3,2,1,0:T(8,128)(2,1)S(1)}, bf16[3,2,64,512]{3,2,1,0:T(8,128)(2,1)S(1)}, u32[]{:S(2)}, u32[]{:S(2)}) collective-permute-start(bf16[3,2,64,512]{3,2,1,0:T(8,128)(2,1)S(1)} %get-tuple-element.12.first), channel_id=1, source_target_pairs={{0,2},{2,0},{4,6},{6,4},{1,3},{3,1},{5,7},{7,5},{8,10},{10,8},{12,... | collective-permute-start | bytes 1179656 | tf_op jit(solution)/shard_map/ppermute | solution.py:334
  25.5 14.5 %all-to-all-start.1 = ((bf16[64,32,128]{2,1,0:T(8,128)(2,1)}), bf16[64,32,128]{2,1,0:T(8,128)(2,1)S(1)}, u32[]{:S(2)}, u32[]{:S(2)}) async-start(bf16[64,32,128]{2,1,0:T(8,128)(2,1)} %get-tuple-element.13), calls=%async_computation.1 | async-start | bytes 1048576 | tf_op jit(solution)/shard_map/all_to_all | solution.py:326
  40.1 0.9 %shard_map.148.first = bf16[2,3,2,64,512]{4,3,2,1,0:T(8,128)(2,1)} custom-call(bf16[3,2,64,512]{3,2,1,0:T(8,128)(2,1)S(1)} %get-tuple-element.12.first, bf16[3,2,64,512]{3,2,1,0:T(8,128)(2,1)S(1)} %collective-permute-done.2.second), custom_call_target="tpu_custom_call" | custom-call | flops 1000000000 | bytes 1572864 | tf_op jit(solution)/shard_map/pallas_call | solution.py:328
  41.0 3.3 %collective-permute-start.3 = (bf16[2,3,2,64,512]{4,3,2,1,0:T(8,128)(2,1)}, bf16[2,3,2,64,512]{4,3,2,1,0:T(8,128)(2,1)}, u32[]{:S(2)}, u32[]{:S(2)}) collective-permute-start(bf16[2,3,2,64,512]{4,3,2,1,0:T(8,128)(2,1)} %shard_map.148.first), channel_id=1, source_target_pairs={{0,6},{2,4},{4,2},{6,0},{1,7},{3,5},{5,3},{7,1},{8,14},{10,12},{12... | collective-permute-start | bytes 2359304 | tf_op jit(solution)/shard_map/ppermute | solution.py:335
  44.3 3.5 %collective-permute-start.5 = (bf16[2,256,512]{2,1,0:T(8,128)(2,1)}, bf16[2,256,512]{2,1,0:T(8,128)(2,1)S(1)}, u32[]{:S(2)}, u32[]{:S(2)}) collective-permute-start(bf16[2,256,512]{2,1,0:T(8,128)(2,1)} %own.1), channel_id=1, source_target_pairs={{1,2},{3,4},{5,6},{7,8},{9,10},{11,12},{13,14},{15,16},{17,18},{19... | collective-permute-start | bytes 1572872 | tf_op jit(solution)/shard_map/ppermute | solution.py:249
  47.8 1.9 %collective-permute-start.4 = (bf16[2,256,512]{2,1,0:T(8,128)(2,1)}, bf16[2,256,512]{2,1,0:T(8,128)(2,1)S(1)}, u32[]{:S(2)}, u32[]{:S(2)}) collective-permute-start(bf16[2,256,512]{2,1,0:T(8,128)(2,1)} %own.1), channel_id=1, source_target_pairs={{0,1},{2,3},{4,5},{6,7},{8,9},{10,11},{12,13},{14,15},{16,17},{18,... | collective-permute-start | bytes 1572872 | tf_op jit(solution)/shard_map/ppermute | solution.py:249
  49.7 6.4 %all-to-all-done.1.boxes = bf16[64,32,128]{2,1,0:T(8,128)(2,1)S(1)} async-done(((bf16[64,32,128]{2,1,0:T(8,128)(2,1)}), bf16[64,32,128]{2,1,0:T(8,128)(2,1)S(1)}, u32[]{:S(2)}, u32[]{:S(2)}) %all-to-all-start.1) | async-done | bytes 524320 | tf_op jit(solution)/shard_map/all_to_all | solution.py:326
  56.2 1.5 %shard_map.149 = bf16[8,64,128]{2,1,0:T(8,128)(2,1)} custom-call(bf16[64,3072]{1,0:T(8,128)(2,1)S(1)} %copy-done.1, bf16[64,32,128]{2,1,0:T(8,128)(2,1)S(1)} %all-to-all-done.1.boxes, s32[1,16]{1,0:T(1,128)S(1)} %copy-done.10, s32[4,8]{1,0:T(4,128)S(1)} %bitcast.6), custom_call_target="tpu_custom_call" | custom-call | flops 50331648 | bytes 524288 | tf_op jit(solution)/shard_map/pallas_call | solution.py:341
  57.7 7.5 %all-to-all-start.2 = ((bf16[8,64,128]{2,1,0:T(8,128)(2,1)}), bf16[8,64,128]{2,1,0:T(8,128)(2,1)S(1)}, u32[]{:S(2)}, u32[]{:S(2)}) async-start(bf16[8,64,128]{2,1,0:T(8,128)(2,1)} %shard_map.149), calls=%async_computation.2 | async-start | bytes 262144 | tf_op jit(solution)/shard_map/all_to_all | solution.py:348
  65.2 5.2 %all-to-all-done.2.after.local_far = bf16[8,64,128]{2,1,0:T(8,128)(2,1)S(1)} async-done(((bf16[8,64,128]{2,1,0:T(8,128)(2,1)}), bf16[8,64,128]{2,1,0:T(8,128)(2,1)S(1)}, u32[]{:S(2)}, u32[]{:S(2)}) %all-to-all-start.2) | async-done | bytes 131104 | tf_op jit(solution)/shard_map/all_to_all | solution.py:348
  70.5 1.5 %shard_map.150 = bf16[4,3,2,64,512]{4,3,2,1,0:T(8,128)(2,1)S(1)} custom-call(bf16[2,3,2,64,512]{4,3,2,1,0:T(8,128)(2,1)} %shard_map.148.first, bf16[2,3,2,64,512]{4,3,2,1,0:T(8,128)(2,1)} %collective-permute-done.3.second, bf16[8,64,128]{2,1,0:T(8,128)(2,1)S(1)} %all-to-all-done.2.after.local_far, bf16[2,256,512]{2,1,0:T(8,128)(2,1)S(1)} %collective-permute-done.4.even, ...), custom_call_target="tpu_custom_call" | custom-call | bytes 3145728 | tf_op jit(solution)/shard_map/pallas_call | solution.py:349
  72.0 2.9 %collective-permute-start.6 = (bf16[4,3,2,64,512]{4,3,2,1,0:T(8,128)(2,1)S(1)}, bf16[4,3,2,64,512]{4,3,2,1,0:T(8,128)(2,1)S(1)}, u32[]{:S(2)}, u32[]{:S(2)}) collective-permute-start(bf16[4,3,2,64,512]{4,3,2,1,0:T(8,128)(2,1)S(1)} %shard_map.150), channel_id=1, source_target_pairs={{0,1},{1,0},{2,3},{3,2},{4,5},{5,4},{6,7},{7,6},{8,9},{9,8},{10,11... | collective-permute-start | bytes 4718600 | tf_op jit(solution)/shard_map/ppermute | solution.py:249
  75.0 2.7 %shard_map.151.near_far = f32[2,256,512]{2,1,0:T(8,128)S(1)} custom-call(bf16[2,256,2048]{2,1,0:T(8,128)(2,1)S(1)} %copy-done.2, bf16[2,256,512]{2,1,0:T(8,128)(2,1)S(1)} %collective-permute-done.4.even, bf16[2,256,512]{2,1,0:T(8,128)(2,1)} %own.1, bf16[2,256,512]{2,1,0:T(8,128)(2,1)S(1)} %collective-permute-done.5.odd, s32[2,8]{1,0:T(2,128)S(1)} %copy-done.9, ...), custom_call_target="tpu_custom_call" | custom-call | flops 1073741824 | bytes 4718592 | tf_op jit(solution)/shard_map/pallas_call | solution.py:361
  77.6 0.3 collective-permute-done.6
  78.0 4.1 %shard_map.152 = bf16[2,256,512]{2,1,0:T(8,128)(2,1)} custom-call(bf16[2,64,2560]{2,1,0:T(8,128)(2,1)S(1)} %copy-done.3, bf16[24,64,512]{2,1,0:T(8,128)(2,1)S(1)} %bitcast.3, bf16[24,64,512]{2,1,0:T(8,128)(2,1)S(1)} %bitcast.4, f32[2,256,512]{2,1,0:T(8,128)S(1)} %shard_map.151.near_far, bf16[2,64,64]{2,1,0:T(8,128)(2,1)S(1)} %copy-done.4, ...), custom_call_target="tpu_custom_call" | custom-call | flops 335544320 | bytes 3145728 | tf_op jit(solution)/shard_map/pallas_call | solution.py:380
  (30 shorter events, 0.1 us)
Async XLA Ops:
  2.1 19.4 %copy-start.5 = (bf16[2,64,512]{2,1,0:T(8,128)(2,1)S(1)}, bf16[2,64,512]{2,1,0:T(8,128)(2,1)}, u32[]{:S(2)}) copy-start(bf16[2,64,512]{2,1,0:T(8,128)(2,1)} %get-tuple-element.11.own) | copy-start | bytes 393220
  2.1 19.4 %collective-permute-start.1 = (bf16[2,64,512]{2,1,0:T(8,128)(2,1)}, bf16[2,64,512]{2,1,0:T(8,128)(2,1)S(1)}, u32[]{:S(2)}, u32[]{:S(2)}) collective-permute-start(bf16[2,64,512]{2,1,0:T(8,128)(2,1)} %get-tuple-element.11.own), channel_id=1, source_target_pairs={{8,16},{24,32},{40,48},{56,64},{72,80},{88,96},{104,112},{120,128}... | collective-permute-start | bytes 393224 | tf_op jit(solution)/shard_map/ppermute | solution.py:249
  2.9 18.6 %collective-permute-start = (bf16[2,64,512]{2,1,0:T(8,128)(2,1)}, bf16[2,64,512]{2,1,0:T(8,128)(2,1)S(1)}, u32[]{:S(2)}, u32[]{:S(2)}) collective-permute-start(bf16[2,64,512]{2,1,0:T(8,128)(2,1)} %get-tuple-element.11.own), channel_id=1, source_target_pairs={{0,8},{16,24},{32,40},{48,56},{64,72},{80,88},{96,104},{112,120},{... | collective-permute-start | bytes 393224 | tf_op jit(solution)/shard_map/ppermute | solution.py:249
  11.1 10.4 %all-to-all-start = ((bf16[8,32,128]{2,1,0:T(8,128)(2,1)}), bf16[8,32,128]{2,1,0:T(8,128)(2,1)S(1)}, u32[]{:S(2)}, u32[]{:S(2)}) async-start(bf16[8,32,128]{2,1,0:T(8,128)(2,1)} %get-tuple-element.10), calls=%async_computation | async-start | bytes 131072 | tf_op jit(solution)/shard_map/all_to_all | solution.py:294
  21.5 1.0 %copy-start = (bf16[64,3072]{1,0:T(8,128)(2,1)S(1)}, bf16[64,3072]{1,0:T(8,128)(2,1)}, u32[]{:S(2)}) copy-start(bf16[64,3072]{1,0:T(8,128)(2,1)} %shard_map.146.before.weights) | copy-start | bytes 1179652
  23.3 16.7 %collective-permute-start.2 = (bf16[3,2,64,512]{3,2,1,0:T(8,128)(2,1)S(1)}, bf16[3,2,64,512]{3,2,1,0:T(8,128)(2,1)S(1)}, u32[]{:S(2)}, u32[]{:S(2)}) collective-permute-start(bf16[3,2,64,512]{3,2,1,0:T(8,128)(2,1)S(1)} %get-tuple-element.12.first), channel_id=1, source_target_pairs={{0,2},{2,0},{4,6},{6,4},{1,3},{3,1},{5,7},{7,5},{8,10},{10,8},{12,... | collective-permute-start | bytes 1179656 | tf_op jit(solution)/shard_map/ppermute | solution.py:334
  25.5 30.6 %all-to-all-start.1 = ((bf16[64,32,128]{2,1,0:T(8,128)(2,1)}), bf16[64,32,128]{2,1,0:T(8,128)(2,1)S(1)}, u32[]{:S(2)}, u32[]{:S(2)}) async-start(bf16[64,32,128]{2,1,0:T(8,128)(2,1)} %get-tuple-element.13), calls=%async_computation.1 | async-start | bytes 1048576 | tf_op jit(solution)/shard_map/all_to_all | solution.py:326
  40.0 16.1 %copy-start.1 = (bf16[64,3072]{1,0:T(8,128)(2,1)S(1)}, bf16[64,3072]{1,0:T(8,128)(2,1)}, u32[]{:S(2)}) copy-start(bf16[64,3072]{1,0:T(8,128)(2,1)} %shard_map.146.before.weights) | copy-start | bytes 1179652
  40.0 16.1 %copy-start.7 = (s32[8,4]{0,1:T(4,128)S(1)}, s32[8,4]{0,1:T(4,128)}, u32[]{:S(2)}) copy-start(s32[8,4]{0,1:T(4,128)} %param.29) | copy-start | bytes 388
  40.1 16.1 %copy-start.10 = (s32[1,16]{1,0:T(1,128)S(1)}, s32[1,16]{1,0:T(1,128)}, u32[]{:S(2)}) copy-start(s32[1,16]{1,0:T(1,128)} %box_partners.1) | copy-start | bytes 196
  41.0 29.5 %collective-permute-start.3 = (bf16[2,3,2,64,512]{4,3,2,1,0:T(8,128)(2,1)}, bf16[2,3,2,64,512]{4,3,2,1,0:T(8,128)(2,1)}, u32[]{:S(2)}, u32[]{:S(2)}) collective-permute-start(bf16[2,3,2,64,512]{4,3,2,1,0:T(8,128)(2,1)} %shard_map.148.first), channel_id=1, source_target_pairs={{0,6},{2,4},{4,2},{6,0},{1,7},{3,5},{5,3},{7,1},{8,14},{10,12},{12... | collective-permute-start | bytes 2359304 | tf_op jit(solution)/shard_map/ppermute | solution.py:335
  44.3 20.9 %collective-permute-start.5 = (bf16[2,256,512]{2,1,0:T(8,128)(2,1)}, bf16[2,256,512]{2,1,0:T(8,128)(2,1)S(1)}, u32[]{:S(2)}, u32[]{:S(2)}) collective-permute-start(bf16[2,256,512]{2,1,0:T(8,128)(2,1)} %own.1), channel_id=1, source_target_pairs={{1,2},{3,4},{5,6},{7,8},{9,10},{11,12},{13,14},{15,16},{17,18},{19... | collective-permute-start | bytes 1572872 | tf_op jit(solution)/shard_map/ppermute | solution.py:249
  47.8 17.4 %collective-permute-start.4 = (bf16[2,256,512]{2,1,0:T(8,128)(2,1)}, bf16[2,256,512]{2,1,0:T(8,128)(2,1)S(1)}, u32[]{:S(2)}, u32[]{:S(2)}) collective-permute-start(bf16[2,256,512]{2,1,0:T(8,128)(2,1)} %own.1), channel_id=1, source_target_pairs={{0,1},{2,3},{4,5},{6,7},{8,9},{10,11},{12,13},{14,15},{16,17},{18,... | collective-permute-start | bytes 1572872 | tf_op jit(solution)/shard_map/ppermute | solution.py:249
  57.7 12.8 %all-to-all-start.2 = ((bf16[8,64,128]{2,1,0:T(8,128)(2,1)}), bf16[8,64,128]{2,1,0:T(8,128)(2,1)S(1)}, u32[]{:S(2)}, u32[]{:S(2)}) async-start(bf16[8,64,128]{2,1,0:T(8,128)(2,1)} %shard_map.149), calls=%async_computation.2 | async-start | bytes 262144 | tf_op jit(solution)/shard_map/all_to_all | solution.py:348
  65.2 9.7 %copy-start.2 = (bf16[2,256,2048]{2,1,0:T(8,128)(2,1)S(1)}, bf16[2,256,2048]{2,1,0:T(8,128)(2,1)}, u32[]{:S(2)}) copy-start(bf16[2,256,2048]{2,1,0:T(8,128)(2,1)} %blocks_far.1) | copy-start | bytes 6291460
  65.2 9.7 %copy-start.9 = (s32[2,8]{1,0:T(2,128)S(1)}, s32[2,8]{1,0:T(2,128)}, u32[]{:S(2)}) copy-start(s32[2,8]{1,0:T(2,128)} %leaves_far.1) | copy-start | bytes 196
  65.2 9.7 %copy-start.12 = (s32[2]{0:T(128)S(1)}, s32[2]{0:T(128)}, u32[]{:S(2)}) copy-start(s32[2]{0:T(128)} %count_far.1) | copy-start | bytes 28
  72.0 6.0 %copy-start.3 = (bf16[2,64,2560]{2,1,0:T(8,128)(2,1)S(1)}, bf16[2,64,2560]{2,1,0:T(8,128)(2,1)}, u32[]{:S(2)}) copy-start(bf16[2,64,2560]{2,1,0:T(8,128)(2,1)} %coupling_far.3) | copy-start | bytes 1966084
  72.0 6.0 %copy-start.4 = (bf16[2,64,64]{2,1,0:T(8,128)(2,1)S(1)}, bf16[2,64,64]{2,1,0:T(8,128)(2,1)}, u32[]{:S(2)}) copy-start(bf16[2,64,64]{2,1,0:T(8,128)(2,1)} %transfer_far.5) | copy-start | bytes 49156
  72.0 6.0 %copy-start.6 = (bf16[2,64,256]{2,1,0:T(8,128)(2,1)S(1)}, bf16[2,64,256]{2,1,0:T(8,128)(2,1)}, u32[]{:S(2)}) copy-start(bf16[2,64,256]{2,1,0:T(8,128)(2,1)} %target_far.1) | copy-start | bytes 196612
  72.0 6.0 %copy-start.8 = (s32[2,40]{1,0:T(2,128)S(1)}, s32[2,40]{1,0:T(2,128)}, u32[]{:S(2)}) copy-start(s32[2,40]{1,0:T(2,128)} %far_leaves_far.1) | copy-start | bytes 964
  72.0 6.0 %copy-start.11 = (s32[2]{0:T(128)S(1)}, s32[2]{0:T(128)}, u32[]{:S(2)}) copy-start(s32[2]{0:T(128)} %far_count_far.1) | copy-start | bytes 28
  72.0 5.9 %collective-permute-start.6 = (bf16[4,3,2,64,512]{4,3,2,1,0:T(8,128)(2,1)S(1)}, bf16[4,3,2,64,512]{4,3,2,1,0:T(8,128)(2,1)S(1)}, u32[]{:S(2)}, u32[]{:S(2)}) collective-permute-start(bf16[4,3,2,64,512]{4,3,2,1,0:T(8,128)(2,1)S(1)} %shard_map.150), channel_id=1, source_target_pairs={{0,1},{1,0},{2,3},{3,2},{4,5},{5,4},{6,7},{7,6},{8,9},{9,8},{10,11... | collective-permute-start | bytes 4718600 | tf_op jit(solution)/shard_map/ppermute | solution.py:249

commit v4 on v3

--- a/solution.py
+++ b/solution.py
@@ -26,7 +26,7 @@
     return lax.dot_general(a, b, (((0,), (0,)), ((), ())), preferred_element_type=F32)
 
 
-def call(body, out_shape, spaces, flops, moved, scratch=(), limit=32 << 20, out_space=VMEM):
+def call(body, out_shape, spaces, flops, moved, scratch=(), limit=16 << 20, out_space=VMEM):
     outs = jax.tree.map(lambda _: pl.BlockSpec(memory_space=out_space), out_shape)
     return pl.pallas_call(
         body,
@@ -157,7 +157,7 @@
             value = window[jnp.where(j < count[leaf], at, blank)]
             term = dot(blocks[leaf, :, j * points : (j + 1) * points], value)
             total = term if total is None else total + term
-        out[leaf] = total
+        out[leaf] = total.astype(BF16)
         stores += load_all((out.at[leaf],), (out_far.at[leaf],), out_sems.at[pl.ds(leaf, 1)])
     for store in stores:
         store.wait()
@@ -228,6 +228,7 @@
                 within = source % group_leaves
                 spot = place(source // group_leaves, box_of) * leaf_dev + within % leaf_dev
                 side, chip = (within // leaf_dev) % 2, (within // (2 * leaf_dev)) ^ chip_of
+                chip = jnp.where(side == 0, chip, (4 - chip) % 4)
                 chip = chip ^ (chip // 2)
                 spot = side * (blank // 2) + chip * 3 * leaf_dev + spot
                 rows.append(skeletons[jnp.where(j < far_count[leaf], spot, blank)])
@@ -324,15 +325,19 @@
         boxes * rows * cols * 2,
     )(arrived, even_skeleton, skeleton, odd_skeleton, weights)
     all_boxes = lax.all_to_all(spread, "boxes", 0, 0, tiled=True)
-    flips = [[(i, i ^ flip) for i in range(chips)] for flip in (1, 3)]
+    ring = [(chip, core) for chip in range(chips) for core in range(cores)]
+    flips = [
+        [(chip * cores + core, (chip ^ flip[core]) * cores + core) for chip, core in ring]
+        for flip in ((1, 3), (3, 1))
+    ]
     pair = call(
         pair_body,
         jax.ShapeDtypeStruct((2,) + trio.shape, BF16),
         [VMEM] * 2,
         HUGE,
         4 * trio.size * 2,
-    )(trio, lax.ppermute(trio, "x", flips[0]))
-    opposite = lax.ppermute(pair, "x", flips[1])
+    )(trio, lax.ppermute(trio, grp, flips[0]))
+    opposite = lax.ppermute(pair, grp, flips[1])
 
     held, _ = lax.optimization_barrier((densities, pair))
     even = swap(held, line, 0)
@@ -360,7 +365,7 @@
 
     near_field = call(
         functools.partial(near_body, device_of),
-        jax.ShapeDtypeStruct((leaf_dev, points, vectors), F32),
+        jax.ShapeDtypeStruct((leaf_dev, points, vectors), BF16),
         [HBM] + [pl.ANY] * 5,
         2 * near_blocks.size * vectors,
         near_blocks.size * 2 + 5 * densities.size * 2,
@@ -369,11 +374,11 @@
             VMEM((3 * leaf_dev + 1, points, vectors), BF16),
             SMEM(near_leaves.shape, jnp.int32),
             SMEM(near_count.shape, jnp.int32),
-            VMEM((leaf_dev, points, vectors), F32),
+            VMEM((leaf_dev, points, vectors), BF16),
             pltpu.SemaphoreType.DMA((5 + leaf_dev,)),
             pltpu.SemaphoreType.DMA((leaf_dev,)),
         ),
-        32 << 20,
+        16 << 20,
         HBM,
     )(near_blocks, even, densities, odd, near_leaves, near_count)
     flat = (chips * 3 * leaf_dev, RANK, vectors)
@@ -386,7 +391,7 @@
         (
             VMEM(far_coupling.shape, BF16),
             VMEM((cores * flat[0] + 1, RANK, vectors), BF16),
-            VMEM(near_field.shape, F32),
+            VMEM(near_field.shape, BF16),
             VMEM(leaf_transfer.shape, BF16),
             VMEM(basis_target.shape, BF16),
             SMEM(far_leaves.shape, jnp.int32),
@@ -396,7 +401,7 @@
             pltpu.SemaphoreType.DMA((9,)),
             pltpu.SemaphoreType.DMA((leaf_dev,)),
         ),
-        32 << 20,
+        16 << 20,
         HBM,
     )(
         far_coupling,

time: 82.8 us -> 83.3 us (level)
  waiting for transfers between devices: 13.5 us -> 15.2 us
  starting transfers between devices: 50.3 us -> 48.9 us
    all_to_all x1, waiting for transfers between devices: 6.43 us -> 8.07 us  [shards(): all_boxes = lax.all_to_all(spread, 'boxes', 0, 0, tiled=True)]
    all_to_all x1, starting transfers between devices: 7.55 us -> 6.16 us  [shards(): local = lax.all_to_all(local, grp, 0, 0, tiled=True)]
where the time goes in v4:
time: 83.3 us; the launch traced here: 82.6 us
  starting transfers between devices  48.9 us (59%)
  Pallas kernels  17.1 us (21%)
  waiting for transfers between devices  15.2 us (18%)
  local copies, waits for them, and re-layouts  1.05 us (1%)
    ppermute x5, starting transfers between devices, swap(): return lax.ppermute(block, axis, pairs + [(b, a) for a, b in pairs])  17.9 us
    all_to_all x1, starting transfers between devices, shards(): all_boxes = lax.all_to_all(spread, 'boxes', 0, 0, tiled=True)  14.5 us
    all_to_all x1, waiting for transfers between devices, shards(): all_boxes = lax.all_to_all(spread, 'boxes', 0, 0, tiled=True)  8.07 us
    all_to_all x1, starting transfers between devices, shards(): local = lax.all_to_all(local, grp, 0, 0, tiled=True)  6.16 us
    all_to_all x1, starting transfers between devices, shards(): arrived = lax.all_to_all(pieces, grp, 0, 0, tiled=True)  5.55 us
    all_to_all x1, waiting for transfers between devices, shards(): local = lax.all_to_all(local, grp, 0, 0, tiled=True)  5.26 us
    pallas_call x1, Pallas kernels, shards(): call(functools.partial(leaf_body, groups * leaf_dev), jax.ShapeDtypeStruc...  4.3 us
    pallas_call x1, Pallas kernels, shards(): call(weight_body, jax.ShapeDtypeStruct((RANK, sources * RANK), BF16), [HB...  3.29 us
  transfers between devices with their start and end apart: 10, of which 4 were waited for; matrix products, arithmetic and copies ran while one was open for 0% of the time, Pallas kernels for 10%

profile of v4, /device:TPU:1, one launch (start us, length us, event | category | flops | bytes accessed | tf_op | source)
XLA Modules:
  0.0 82.6 jit_solution(1803452713616876172)
XLA Ops:
  0.0 2.1 %shard_map.145 = (bf16[2,64,512]{2,1,0:T(8,128)(2,1)}, bf16[8,32,128]{2,1,0:T(8,128)(2,1)}) custom-call(bf16[2,64,256]{2,1,0:T(8,128)(2,1)} %basis_far.1, bf16[2,256,512]{2,1,0:T(8,128)(2,1)} %own.1, bf16[2,64,64]{2,1,0:T(8,128)(2,1)} %transfer_far.5), custom_call_target="tpu_custom_call" | custom-call | flops 41943040 | bytes 524288 | tf_op jit(solution)/shard_map/pallas_call | solution.py:278
  2.1 0.0 copy-start.5
  2.1 0.8 collective-permute-start.1
  2.9 8.2 %collective-permute-start = (bf16[2,64,512]{2,1,0:T(8,128)(2,1)}, bf16[2,64,512]{2,1,0:T(8,128)(2,1)S(1)}, u32[]{:S(2)}, u32[]{:S(2)}) collective-permute-start(bf16[2,64,512]{2,1,0:T(8,128)(2,1)} %get-tuple-element.11.own), channel_id=1, source_target_pairs={{0,8},{16,24},{32,40},{48,56},{64,72},{80,88},{96,104},{112,120},{... | collective-permute-start | bytes 393224 | tf_op jit(solution)/shard_map/ppermute | solution.py:250
  11.1 5.5 %all-to-all-start = ((bf16[8,32,128]{2,1,0:T(8,128)(2,1)}), bf16[8,32,128]{2,1,0:T(8,128)(2,1)S(1)}, u32[]{:S(2)}, u32[]{:S(2)}) async-start(bf16[8,32,128]{2,1,0:T(8,128)(2,1)} %get-tuple-element.10), calls=%async_computation | async-start | bytes 131072 | tf_op jit(solution)/shard_map/all_to_all | solution.py:295
  16.6 3.3 %shard_map.146.before.weights = bf16[64,3072]{1,0:T(8,128)(2,1)} custom-call(bf16[1,64,1024]{2,1,0:T(8,128)(2,1)} %coupling_far.2, bf16[64,64,64]{2,1,0:T(8,128)(2,1)} %transfer_far.4, bf16[8,64,256]{2,1,0:T(8,128)(2,1)} %top_far.1, s32[4,8]{1,0:T(4,128)} %bitcast.5), custom_call_target="tpu_custom_call" | custom-call | flops 25165824 | bytes 524288 | tf_op jit(solution)/shard_map/pallas_call | solution.py:302
  19.9 1.5 %all-to-all-done.arrived = bf16[8,32,128]{2,1,0:T(8,128)(2,1)S(1)} async-done(((bf16[8,32,128]{2,1,0:T(8,128)(2,1)}), bf16[8,32,128]{2,1,0:T(8,128)(2,1)S(1)}, u32[]{:S(2)}, u32[]{:S(2)}) %all-to-all-start) | async-done | bytes 65568 | tf_op jit(solution)/shard_map/all_to_all | solution.py:295
  21.5 1.0 %copy-done = bf16[64,3072]{1,0:T(8,128)(2,1)S(1)} copy-done((bf16[64,3072]{1,0:T(8,128)(2,1)S(1)}, bf16[64,3072]{1,0:T(8,128)(2,1)}, u32[]{:S(2)}) %copy-start) | copy-done | bytes 393240
  22.5 0.9 %shard_map.147 = (bf16[64,32,128]{2,1,0:T(8,128)(2,1)}, bf16[3,2,64,512]{3,2,1,0:T(8,128)(2,1)S(1)}) custom-call(bf16[8,32,128]{2,1,0:T(8,128)(2,1)S(1)} %all-to-all-done.arrived, bf16[2,64,512]{2,1,0:T(8,128)(2,1)S(1)} %collective-permute-done.even, bf16[2,64,512]{2,1,0:T(8,128)(2,1)S(1)} %copy-done.5, bf16[2,64,512]{2,1,0:T(8,128)(2,1)S(1)} %collective-permute-done.1.odd, ...), custom_call_target="tpu_custom_call" | custom-call | flops 32768 | bytes 524288 | tf_op jit(solution)/shard_map/pallas_call | solution.py:317
  23.3 3.0 %collective-permute-start.2 = (bf16[3,2,64,512]{3,2,1,0:T(8,128)(2,1)S(1)}, bf16[3,2,64,512]{3,2,1,0:T(8,128)(2,1)S(1)}, u32[]{:S(2)}, u32[]{:S(2)}) collective-permute-start(bf16[3,2,64,512]{3,2,1,0:T(8,128)(2,1)S(1)} %get-tuple-element.12.first), channel_id=1, source_target_pairs={{0,2},{1,7},{2,0},{3,5},{4,6},{5,3},{6,4},{7,1},{8,10},{9,15},{10,... | collective-permute-start | bytes 1179656 | tf_op jit(solution)/shard_map/ppermute | solution.py:339
  26.3 14.5 %all-to-all-start.1 = ((bf16[64,32,128]{2,1,0:T(8,128)(2,1)}), bf16[64,32,128]{2,1,0:T(8,128)(2,1)S(1)}, u32[]{:S(2)}, u32[]{:S(2)}) async-start(bf16[64,32,128]{2,1,0:T(8,128)(2,1)} %get-tuple-element.13), calls=%async_computation.1 | async-start | bytes 1048576 | tf_op jit(solution)/shard_map/all_to_all | solution.py:327
  40.9 0.9 %shard_map.148.first = bf16[2,3,2,64,512]{4,3,2,1,0:T(8,128)(2,1)} custom-call(bf16[3,2,64,512]{3,2,1,0:T(8,128)(2,1)S(1)} %get-tuple-element.12.first, bf16[3,2,64,512]{3,2,1,0:T(8,128)(2,1)S(1)} %collective-permute-done.2.second), custom_call_target="tpu_custom_call" | custom-call | flops 1000000000 | bytes 1572864 | tf_op jit(solution)/shard_map/pallas_call | solution.py:333
  41.8 1.9 %collective-permute-start.3 = (bf16[2,3,2,64,512]{4,3,2,1,0:T(8,128)(2,1)}, bf16[2,3,2,64,512]{4,3,2,1,0:T(8,128)(2,1)}, u32[]{:S(2)}, u32[]{:S(2)}) collective-permute-start(bf16[2,3,2,64,512]{4,3,2,1,0:T(8,128)(2,1)} %shard_map.148.first), channel_id=1, source_target_pairs={{0,6},{1,3},{2,4},{3,1},{4,2},{5,7},{6,0},{7,5},{8,14},{9,11},{10,... | collective-permute-start | bytes 2359304 | tf_op jit(solution)/shard_map/ppermute | solution.py:340
  43.7 4.1 %collective-permute-start.5 = (bf16[2,256,512]{2,1,0:T(8,128)(2,1)}, bf16[2,256,512]{2,1,0:T(8,128)(2,1)S(1)}, u32[]{:S(2)}, u32[]{:S(2)}) collective-permute-start(bf16[2,256,512]{2,1,0:T(8,128)(2,1)} %own.1), channel_id=1, source_target_pairs={{1,2},{3,4},{5,6},{7,8},{9,10},{11,12},{13,14},{15,16},{17,18},{19... | collective-permute-start | bytes 1572872 | tf_op jit(solution)/shard_map/ppermute | solution.py:250
  47.8 1.9 %collective-permute-start.4 = (bf16[2,256,512]{2,1,0:T(8,128)(2,1)}, bf16[2,256,512]{2,1,0:T(8,128)(2,1)S(1)}, u32[]{:S(2)}, u32[]{:S(2)}) collective-permute-start(bf16[2,256,512]{2,1,0:T(8,128)(2,1)} %own.1), channel_id=1, source_target_pairs={{0,1},{2,3},{4,5},{6,7},{8,9},{10,11},{12,13},{14,15},{16,17},{18,... | collective-permute-start | bytes 1572872 | tf_op jit(solution)/shard_map/ppermute | solution.py:250
  49.7 8.1 %all-to-all-done.1.boxes = bf16[64,32,128]{2,1,0:T(8,128)(2,1)S(1)} async-done(((bf16[64,32,128]{2,1,0:T(8,128)(2,1)}), bf16[64,32,128]{2,1,0:T(8,128)(2,1)S(1)}, u32[]{:S(2)}, u32[]{:S(2)}) %all-to-all-start.1) | async-done | bytes 524320 | tf_op jit(solution)/shard_map/all_to_all | solution.py:327
  57.8 1.5 %shard_map.149 = bf16[8,64,128]{2,1,0:T(8,128)(2,1)} custom-call(bf16[64,3072]{1,0:T(8,128)(2,1)S(1)} %copy-done.1, bf16[64,32,128]{2,1,0:T(8,128)(2,1)S(1)} %all-to-all-done.1.boxes, s32[1,16]{1,0:T(1,128)S(1)} %copy-done.10, s32[4,8]{1,0:T(4,128)S(1)} %bitcast.6), custom_call_target="tpu_custom_call" | custom-call | flops 50331648 | bytes 524288 | tf_op jit(solution)/shard_map/pallas_call | solution.py:346
  59.3 6.2 %all-to-all-start.2 = ((bf16[8,64,128]{2,1,0:T(8,128)(2,1)}), bf16[8,64,128]{2,1,0:T(8,128)(2,1)S(1)}, u32[]{:S(2)}, u32[]{:S(2)}) async-start(bf16[8,64,128]{2,1,0:T(8,128)(2,1)} %shard_map.149), calls=%async_computation.2 | async-start | bytes 262144 | tf_op jit(solution)/shard_map/all_to_all | solution.py:353
  65.5 5.3 %all-to-all-done.2.after.local_far = bf16[8,64,128]{2,1,0:T(8,128)(2,1)S(1)} async-done(((bf16[8,64,128]{2,1,0:T(8,128)(2,1)}), bf16[8,64,128]{2,1,0:T(8,128)(2,1)S(1)}, u32[]{:S(2)}, u32[]{:S(2)}) %all-to-all-start.2) | async-done | bytes 131104 | tf_op jit(solution)/shard_map/all_to_all | solution.py:353
  70.8 1.5 %shard_map.150 = bf16[4,3,2,64,512]{4,3,2,1,0:T(8,128)(2,1)S(1)} custom-call(bf16[2,3,2,64,512]{4,3,2,1,0:T(8,128)(2,1)} %shard_map.148.first, bf16[2,3,2,64,512]{4,3,2,1,0:T(8,128)(2,1)} %collective-permute-done.3.second, bf16[8,64,128]{2,1,0:T(8,128)(2,1)S(1)} %all-to-all-done.2.after.local_far, bf16[2,256,512]{2,1,0:T(8,128)(2,1)S(1)} %collective-permute-done.4.even, ...), custom_call_target="tpu_custom_call" | custom-call | bytes 3145728 | tf_op jit(solution)/shard_map/pallas_call | solution.py:354
  72.3 2.9 %collective-permute-start.6 = (bf16[4,3,2,64,512]{4,3,2,1,0:T(8,128)(2,1)S(1)}, bf16[4,3,2,64,512]{4,3,2,1,0:T(8,128)(2,1)S(1)}, u32[]{:S(2)}, u32[]{:S(2)}) collective-permute-start(bf16[4,3,2,64,512]{4,3,2,1,0:T(8,128)(2,1)S(1)} %shard_map.150), channel_id=1, source_target_pairs={{0,1},{1,0},{2,3},{3,2},{4,5},{5,4},{6,7},{7,6},{8,9},{9,8},{10,11... | collective-permute-start | bytes 4718600 | tf_op jit(solution)/shard_map/ppermute | solution.py:250
  75.2 2.6 %shard_map.151.near_far = bf16[2,256,512]{2,1,0:T(8,128)(2,1)S(1)} custom-call(bf16[2,256,2048]{2,1,0:T(8,128)(2,1)S(1)} %copy-done.2, bf16[2,256,512]{2,1,0:T(8,128)(2,1)S(1)} %collective-permute-done.4.even, bf16[2,256,512]{2,1,0:T(8,128)(2,1)} %own.1, bf16[2,256,512]{2,1,0:T(8,128)(2,1)S(1)} %collective-permute-done.5.odd, s32[2,8]{1,0:T(2,128)S(1)} %copy-done.8, ...), custom_call_target="tpu_custom_call" | custom-call | flops 1073741824 | bytes 4718592 | tf_op jit(solution)/shard_map/pallas_call | solution.py:366
  77.9 0.3 collective-permute-done.6
  78.3 4.3 %shard_map.152 = bf16[2,256,512]{2,1,0:T(8,128)(2,1)} custom-call(bf16[2,64,2560]{2,1,0:T(8,128)(2,1)S(1)} %copy-done.3, bf16[24,64,512]{2,1,0:T(8,128)(2,1)S(1)} %bitcast.3, bf16[24,64,512]{2,1,0:T(8,128)(2,1)S(1)} %bitcast.4, bf16[2,256,512]{2,1,0:T(8,128)(2,1)S(1)} %shard_map.151.near_far, bf16[2,64,64]{2,1,0:T(8,128)(2,1)S(1)} %copy-done.4, ...), custom_call_target="tpu_custom_call" | custom-call | flops 335544320 | bytes 3145728 | tf_op jit(solution)/shard_map/pallas_call | solution.py:385
  (30 shorter events, 0.1 us)
Async XLA Ops:
  2.1 19.4 %copy-start.5 = (bf16[2,64,512]{2,1,0:T(8,128)(2,1)S(1)}, bf16[2,64,512]{2,1,0:T(8,128)(2,1)}, u32[]{:S(2)}) copy-start(bf16[2,64,512]{2,1,0:T(8,128)(2,1)} %get-tuple-element.11.own) | copy-start | bytes 393220
  2.1 19.4 %collective-permute-start.1 = (bf16[2,64,512]{2,1,0:T(8,128)(2,1)}, bf16[2,64,512]{2,1,0:T(8,128)(2,1)S(1)}, u32[]{:S(2)}, u32[]{:S(2)}) collective-permute-start(bf16[2,64,512]{2,1,0:T(8,128)(2,1)} %get-tuple-element.11.own), channel_id=1, source_target_pairs={{8,16},{24,32},{40,48},{56,64},{72,80},{88,96},{104,112},{120,128}... | collective-permute-start | bytes 393224 | tf_op jit(solution)/shard_map/ppermute | solution.py:250
  2.9 18.6 %collective-permute-start = (bf16[2,64,512]{2,1,0:T(8,128)(2,1)}, bf16[2,64,512]{2,1,0:T(8,128)(2,1)S(1)}, u32[]{:S(2)}, u32[]{:S(2)}) collective-permute-start(bf16[2,64,512]{2,1,0:T(8,128)(2,1)} %get-tuple-element.11.own), channel_id=1, source_target_pairs={{0,8},{16,24},{32,40},{48,56},{64,72},{80,88},{96,104},{112,120},{... | collective-permute-start | bytes 393224 | tf_op jit(solution)/shard_map/ppermute | solution.py:250
  11.1 10.4 %all-to-all-start = ((bf16[8,32,128]{2,1,0:T(8,128)(2,1)}), bf16[8,32,128]{2,1,0:T(8,128)(2,1)S(1)}, u32[]{:S(2)}, u32[]{:S(2)}) async-start(bf16[8,32,128]{2,1,0:T(8,128)(2,1)} %get-tuple-element.10), calls=%async_computation | async-start | bytes 131072 | tf_op jit(solution)/shard_map/all_to_all | solution.py:295
  21.5 1.0 %copy-start = (bf16[64,3072]{1,0:T(8,128)(2,1)S(1)}, bf16[64,3072]{1,0:T(8,128)(2,1)}, u32[]{:S(2)}) copy-start(bf16[64,3072]{1,0:T(8,128)(2,1)} %shard_map.146.before.weights) | copy-start | bytes 1179652
  23.3 17.5 %collective-permute-start.2 = (bf16[3,2,64,512]{3,2,1,0:T(8,128)(2,1)S(1)}, bf16[3,2,64,512]{3,2,1,0:T(8,128)(2,1)S(1)}, u32[]{:S(2)}, u32[]{:S(2)}) collective-permute-start(bf16[3,2,64,512]{3,2,1,0:T(8,128)(2,1)S(1)} %get-tuple-element.12.first), channel_id=1, source_target_pairs={{0,2},{1,7},{2,0},{3,5},{4,6},{5,3},{6,4},{7,1},{8,10},{9,15},{10,... | collective-permute-start | bytes 1179656 | tf_op jit(solution)/shard_map/ppermute | solution.py:339
  26.3 31.5 %all-to-all-start.1 = ((bf16[64,32,128]{2,1,0:T(8,128)(2,1)}), bf16[64,32,128]{2,1,0:T(8,128)(2,1)S(1)}, u32[]{:S(2)}, u32[]{:S(2)}) async-start(bf16[64,32,128]{2,1,0:T(8,128)(2,1)} %get-tuple-element.13), calls=%async_computation.1 | async-start | bytes 1048576 | tf_op jit(solution)/shard_map/all_to_all | solution.py:327
  40.8 17.0 %copy-start.1 = (bf16[64,3072]{1,0:T(8,128)(2,1)S(1)}, bf16[64,3072]{1,0:T(8,128)(2,1)}, u32[]{:S(2)}) copy-start(bf16[64,3072]{1,0:T(8,128)(2,1)} %shard_map.146.before.weights) | copy-start | bytes 1179652
  40.8 17.0 %copy-start.7 = (s32[8,4]{0,1:T(4,128)S(1)}, s32[8,4]{0,1:T(4,128)}, u32[]{:S(2)}) copy-start(s32[8,4]{0,1:T(4,128)} %param.29) | copy-start | bytes 388
  40.8 17.0 %copy-start.10 = (s32[1,16]{1,0:T(1,128)S(1)}, s32[1,16]{1,0:T(1,128)}, u32[]{:S(2)}) copy-start(s32[1,16]{1,0:T(1,128)} %box_partners.1) | copy-start | bytes 196
  41.8 29.0 %collective-permute-start.3 = (bf16[2,3,2,64,512]{4,3,2,1,0:T(8,128)(2,1)}, bf16[2,3,2,64,512]{4,3,2,1,0:T(8,128)(2,1)}, u32[]{:S(2)}, u32[]{:S(2)}) collective-permute-start(bf16[2,3,2,64,512]{4,3,2,1,0:T(8,128)(2,1)} %shard_map.148.first), channel_id=1, source_target_pairs={{0,6},{1,3},{2,4},{3,1},{4,2},{5,7},{6,0},{7,5},{8,14},{9,11},{10,... | collective-permute-start | bytes 2359304 | tf_op jit(solution)/shard_map/ppermute | solution.py:340
  43.7 21.8 %collective-permute-start.5 = (bf16[2,256,512]{2,1,0:T(8,128)(2,1)}, bf16[2,256,512]{2,1,0:T(8,128)(2,1)S(1)}, u32[]{:S(2)}, u32[]{:S(2)}) collective-permute-start(bf16[2,256,512]{2,1,0:T(8,128)(2,1)} %own.1), channel_id=1, source_target_pairs={{1,2},{3,4},{5,6},{7,8},{9,10},{11,12},{13,14},{15,16},{17,18},{19... | collective-permute-start | bytes 1572872 | tf_op jit(solution)/shard_map/ppermute | solution.py:250
  47.8 17.7 %collective-permute-start.4 = (bf16[2,256,512]{2,1,0:T(8,128)(2,1)}, bf16[2,256,512]{2,1,0:T(8,128)(2,1)S(1)}, u32[]{:S(2)}, u32[]{:S(2)}) collective-permute-start(bf16[2,256,512]{2,1,0:T(8,128)(2,1)} %own.1), channel_id=1, source_target_pairs={{0,1},{2,3},{4,5},{6,7},{8,9},{10,11},{12,13},{14,15},{16,17},{18,... | collective-permute-start | bytes 1572872 | tf_op jit(solution)/shard_map/ppermute | solution.py:250
  59.3 11.5 %all-to-all-start.2 = ((bf16[8,64,128]{2,1,0:T(8,128)(2,1)}), bf16[8,64,128]{2,1,0:T(8,128)(2,1)S(1)}, u32[]{:S(2)}, u32[]{:S(2)}) async-start(bf16[8,64,128]{2,1,0:T(8,128)(2,1)} %shard_map.149), calls=%async_computation.2 | async-start | bytes 262144 | tf_op jit(solution)/shard_map/all_to_all | solution.py:353
  65.5 9.7 %copy-start.2 = (bf16[2,256,2048]{2,1,0:T(8,128)(2,1)S(1)}, bf16[2,256,2048]{2,1,0:T(8,128)(2,1)}, u32[]{:S(2)}) copy-start(bf16[2,256,2048]{2,1,0:T(8,128)(2,1)} %blocks_far.1) | copy-start | bytes 6291460
  65.5 9.8 %copy-start.8 = (s32[2,8]{1,0:T(2,128)S(1)}, s32[2,8]{1,0:T(2,128)}, u32[]{:S(2)}) copy-start(s32[2,8]{1,0:T(2,128)} %leaves_far.1) | copy-start | bytes 196
  65.5 9.8 %copy-start.11 = (s32[2]{0:T(128)S(1)}, s32[2]{0:T(128)}, u32[]{:S(2)}) copy-start(s32[2]{0:T(128)} %count_far.1) | copy-start | bytes 28
  72.2 6.0 %copy-start.3 = (bf16[2,64,2560]{2,1,0:T(8,128)(2,1)S(1)}, bf16[2,64,2560]{2,1,0:T(8,128)(2,1)}, u32[]{:S(2)}) copy-start(bf16[2,64,2560]{2,1,0:T(8,128)(2,1)} %coupling_far.3) | copy-start | bytes 1966084
  72.3 6.0 %copy-start.4 = (bf16[2,64,64]{2,1,0:T(8,128)(2,1)S(1)}, bf16[2,64,64]{2,1,0:T(8,128)(2,1)}, u32[]{:S(2)}) copy-start(bf16[2,64,64]{2,1,0:T(8,128)(2,1)} %transfer_far.5) | copy-start | bytes 49156
  72.3 6.0 %copy-start.6 = (bf16[2,64,256]{2,1,0:T(8,128)(2,1)S(1)}, bf16[2,64,256]{2,1,0:T(8,128)(2,1)}, u32[]{:S(2)}) copy-start(bf16[2,64,256]{2,1,0:T(8,128)(2,1)} %target_far.1) | copy-start | bytes 196612
  72.3 6.0 %copy-start.9 = (s32[2,40]{1,0:T(2,128)S(1)}, s32[2,40]{1,0:T(2,128)}, u32[]{:S(2)}) copy-start(s32[2,40]{1,0:T(2,128)} %far_leaves_far.1) | copy-start | bytes 964
  72.3 6.0 %copy-start.12 = (s32[2]{0:T(128)S(1)}, s32[2]{0:T(128)}, u32[]{:S(2)}) copy-start(s32[2]{0:T(128)} %far_count_far.1) | copy-start | bytes 28
  72.3 5.9 %collective-permute-start.6 = (bf16[4,3,2,64,512]{4,3,2,1,0:T(8,128)(2,1)S(1)}, bf16[4,3,2,64,512]{4,3,2,1,0:T(8,128)(2,1)S(1)}, u32[]{:S(2)}, u32[]{:S(2)}) collective-permute-start(bf16[4,3,2,64,512]{4,3,2,1,0:T(8,128)(2,1)S(1)} %shard_map.150), channel_id=1, source_target_pairs={{0,1},{1,0},{2,3},{3,2},{4,5},{5,4},{6,7},{7,6},{8,9},{9,8},{10,11... | collective-permute-start | bytes 4718600 | tf_op jit(solution)/shard_map/ppermute | solution.py:250
